TPU v7x, 512 devices: a whole 4x8x8 slice. The times are simulated.
512 devices in a mesh: replica: 32 (over x_lo, y, core), tensor: 16 (over z, x_hi).
Axes of the slice: x: 4 (x_hi: 2, x_lo: 2; x = x_hi * 2 + x_lo), y: 8, z: 8, core: 2. Of those that a mesh axis runs over, the one named last changes fastest.
Arguments:
- hidden: bfloat16 [2, 1, 16384, 12288], P(None, None, 'replica', 'tensor'), may hold values from -6 to 6
- queries: bfloat16 [2, 1, 16384, 6144], P(None, None, ('replica', 'tensor')), may hold values from -160 to 160
- kv_cache: bfloat16 [1, 16384, 16, 1024], P(None, ('replica', 'tensor')), may hold values from -6 to 6
- lengths: int32 [16384], P(('replica', 'tensor')), may hold values from 2 to 16, as said below
- versions: int32 [32, 1], replicated, may hold values from 0 to 1, as said below
- resident: bfloat16 [1, 12288, 1024], P(None, 'tensor'), may hold values from -0.0546875 to 0.0546875
- update: bfloat16 [1, 12288, 1024], P(None, ('tensor', 'replica')), may hold values from -0.0546875 to 0.0546875
Outputs:
- attended: bfloat16 [2, 1, 16384, 6144], P(None, None, ('replica', 'tensor'))
Inputs may be any that keep to these rules, and one draw needn't show every extreme that they name: `lengths`: some row has exactly 16. `versions`: in every layer some replica runs version 1 and some runs version 0.
All inputs are finite; a program needn't handle non-finite values.
Results may differ from a plain program's by a relative error of at most 0.0054.
Values may be sent and summed in bfloat16 or wider, within the bound.
No kernel may reach another device: no remote copies, remote signals or barrier semaphores. Data moves between devices by JAX's collectives and lax.ppermute only.
A program may use at most 64 MiB of HBM per device.

v0:
```python
import math

import jax
import jax.numpy as jnp
from jax import lax
from jax.sharding import PartitionSpec as P

HEAD = 128
QPK = 12
KVH = 4


THETA = 1000000.0


def rotate_keys(kv_sum, positions):
    lead_shape = kv_sum.shape[:-1]
    key_width = KVH * HEAD
    key_part = kv_sum[..., :key_width].reshape(lead_shape + (KVH, HEAD))
    half_head = HEAD // 2
    inverse = THETA ** (-(jnp.arange(half_head, dtype=jnp.float32) * 2.0 / HEAD))
    angles = positions[..., None, None] * inverse
    cosine_table = jnp.cos(angles)
    sine_table = jnp.sin(angles)
    front_half = key_part[..., :half_head]
    back_half = key_part[..., half_head:]
    rotated = jnp.concatenate(
        [
            front_half * cosine_table - back_half * sine_table,
            back_half * cosine_table + front_half * sine_table,
        ],
        -1,
    )
    return jnp.concatenate(
        [rotated.reshape(lead_shape + (key_width,)), kv_sum[..., key_width:]], -1
    )


def attend(query_rows, cache_rows, kv_new, lengths):
    step_count = query_rows.shape[0]
    row_count = query_rows.shape[1]
    slot_count = cache_rows.shape[1]
    key_width = KVH * HEAD
    query_heads = query_rows.reshape(step_count, row_count, KVH, QPK, HEAD)
    cache_keys = cache_rows[:, :, :key_width].reshape(row_count, slot_count, KVH, HEAD)
    cache_values = cache_rows[:, :, key_width:].reshape(row_count, slot_count, KVH, HEAD)
    new_keys = kv_new[..., :key_width].reshape(step_count, row_count, KVH, HEAD)
    new_values = kv_new[..., key_width:].reshape(step_count, row_count, KVH, HEAD)
    score_scale = 1.0 / math.sqrt(HEAD)
    cache_scores = (
        jnp.einsum("srgjd,rpgd->srgjp", query_heads, cache_keys, preferred_element_type=jnp.float32)
        * score_scale
    )
    new_scores = (
        jnp.einsum("srgjd,trgd->srgjt", query_heads, new_keys, preferred_element_type=jnp.float32)
        * score_scale
    )
    filled = jnp.arange(slot_count, dtype=jnp.int32)[None, :] < lengths[:, None]
    cache_scores = jnp.where(filled[None, :, None, None, :], cache_scores, -1e30)
    causal = (
        jnp.arange(step_count, dtype=jnp.int32)[None, :]
        <= jnp.arange(step_count, dtype=jnp.int32)[:, None]
    )
    new_scores = jnp.where(causal[:, None, None, None, :], new_scores, -1e30)
    highest = jnp.maximum(jnp.max(cache_scores, -1), jnp.max(new_scores, -1))[..., None]
    cache_exp = jnp.exp(cache_scores - highest)
    new_exp = jnp.exp(new_scores - highest)
    denominator = jnp.sum(cache_exp, -1, keepdims=True) + jnp.sum(new_exp, -1, keepdims=True)
    cache_weights = (cache_exp / denominator).astype(jnp.bfloat16)
    new_weights = (new_exp / denominator).astype(jnp.bfloat16)
    attended = jnp.einsum(
        "srgjp,rpgd->srgjd", cache_weights, cache_values, preferred_element_type=jnp.float32
    )
    attended = attended + jnp.einsum(
        "srgjt,trgd->srgjd", new_weights, new_values, preferred_element_type=jnp.float32
    )
    return attended.reshape(step_count, row_count, KVH * QPK * HEAD).astype(jnp.bfloat16)


def per_device(hidden, queries, kv_cache, lengths, versions, resident, update):
    replica_index = lax.axis_index("replica")
    step_count, layer_count, row_count, shard_width = hidden.shape
    kv_width = resident.shape[2]
    flattened = hidden[:, 0].reshape(step_count * row_count, shard_width)
    old_rows = resident[0]
    new_piece = update[0]
    version = lax.dynamic_index_in_dim(versions[:, 0], replica_index, 0, keepdims=False)
    chosen = jnp.where(
        version == 1, lax.all_gather(new_piece, "replica", axis=0, tiled=True), old_rows
    )
    partial_kv = jnp.dot(flattened, chosen, preferred_element_type=jnp.float32)
    summed = lax.psum_scatter(
        partial_kv.reshape(step_count, row_count, kv_width),
        "tensor",
        scatter_dimension=1,
        tiled=True,
    )
    positions = (lengths[None, :] + jnp.arange(step_count, dtype=jnp.int32)[:, None]).astype(
        jnp.float32
    )
    kv_new = rotate_keys(summed, positions).astype(jnp.bfloat16)
    results = [attend(queries[:, 0], kv_cache[0], kv_new, lengths)]
    return jnp.stack(results, 1)


def solution(mesh):
    placed = (
        P(None, None, "replica", "tensor"),
        P(None, None, ("replica", "tensor"), None),
        P(None, ("replica", "tensor"), None, None),
        P(("replica", "tensor")),
        P(),
        P(None, "tensor", None),
        P(None, ("tensor", "replica"), None),
    )
    return jax.shard_map(
        per_device,
        mesh=mesh,
        in_specs=placed,
        out_specs=P(None, None, ("replica", "tensor"), None),
        check_vma=False,
    )
```

profile of v0, /device:TPU:8, one launch (start us, length us, event | category | flops | bytes accessed | tf_op | source)
XLA Modules:
  0.0 319.5 jit_solution(16620284659583717265)
XLA Ops:
  6.5 0.7 all-gather.3.cloned.1.call-update
  7.3 1.2 fusion.31
  8.6 71.5 %all-gather.3.cloned.1.call-done = bf16[1,768,1024]{2,1,0:T(8,128)(2,1)} async-done(((bf16[1,24,1024]{2,1,0:T(8,128)(2,1)}), bf16[1,768,1024]{2,1,0:T(8,128)(2,1)}) %all-gather.3.cloned.1.call-update) | async-done | bytes 1572880 | tf_op jit(solution)/shard_map/all_gather | solution.py:89
  80.0 5.8 %fusion.3 = f32[1024,1024]{0,1:T(8,128)} fusion(bf16[1024,768]{1,0:T(8,128)(2,1)S(1)} %bitcast.43, bf16[1,768,1024]{2,1,0:T(8,128)(2,1)} %all-gather.3.cloned.1.call-done, bf16[1,768,1024]{2,1,0:T(8,128)(2,1)} %param.12, pred[]{:T(512)} %bitcast.3), kind=kOutput, calls=%fused_computation.8 | convolution fusion | flops 1611399168 | bytes 8912897 | tf_op jit(solution)/shard_map/dot_general | solution.py:91
  85.9 1.1 copy-done.4
  87.0 1.5 reshape_squeeze.6
  88.5 1.3 fusion.29
  89.8 0.9 reshape.110
  90.7 0.1 reshape.113
  91.0 0.5 multiply_cosine_fusion
  91.6 6.1 %bitcast_reduce_fusion = (f32[2,32,4,12]{3,0,2,1:T(2,128)}, f32[32,4,16,2,12]{4,2,3,1,0:T(8,128)}) fusion(pred[32,16]{1,0:T(8,128)(4,1)S(1)} %iota_compare_fusion, bf16[2,32,4,12,128]{4,3,2,1,0:T(8,128)(2,1)} %reshape_squeeze.6, bf16[32,16,4,128,1]{3,2,1,0,4:T(4,128)(2,1)} %bitcast.47), kind=kOutput, calls=%fused_computation.3 | convolution fusion | flops 12727296 | bytes 1520128 | tf_op jit(solution)/shard_map/srgjd,rpgd->srgjp/dot_general | solution.py:51
  97.6 203.9 %reduce-scatter.2.cloned.1.call-done = f32[2,32,1024]{2,1,0:T(8,128)} async-done(((f32[2,512,1024]{2,1,0:T(8,128)}), f32[2,32,1024]{2,1,0:T(8,128)}) %reduce-scatter.2.cloned.1.call-update) | async-done | bytes 262160 | tf_op jit(solution)/shard_map/reduce_scatter | solution.py:92
  301.5 0.9 slice.28
  302.5 0.1 fusion.30
  302.7 0.3 subtract_convert_fusion
  302.9 2.7 fusion.32
  305.7 0.5 fusion.19
  306.2 0.9 fusion.2
  307.2 0.9 slice.34
  308.2 0.6 fusion.20
  308.8 1.0 copy-done.2
  309.8 1.2 fusion
  311.0 0.3 copy.19
  311.3 1.4 convert_element_type.31
  (23 shorter events, 0.5 us)
Async XLA Ops:
  6.5 73.5 %copy-start = (bf16[2,1,512,768]{3,2,1,0:T(8,128)(2,1)S(1)}, bf16[2,1,512,768]{3,2,1,0:T(8,128)(2,1)}, u32[]{:S(2)}) copy-start(bf16[2,1,512,768]{3,2,1,0:T(8,128)(2,1)} %param.7) | copy-start | bytes 4718596
  6.5 73.5 %all-gather.3.cloned.1.call-start = ((), (), s32[]{:S(2)}) async-start(), calls=%async_computation.2 | async-start | bytes 1622016 | tf_op jit(solution)/shard_map/all_gather | solution.py:89
  7.3 294.3 %reduce-scatter.2.cloned.1.call-start = ((), (), s32[]{:S(2)}) async-start(), calls=%async_computation.1 | async-start | bytes 4456448 | tf_op jit(solution)/shard_map/reduce_scatter | solution.py:92
  85.8 1.1 copy-start.4
  88.5 2.4 copy-start.6
  91.6 211.4 %copy-start.3 = (bf16[2,32,4,12,128]{4,3,2,1,0:T(8,128)(2,1)S(1)}, bf16[2,32,4,12,128]{4,3,2,1,0:T(8,128)(2,1)}, u32[]{:S(2)}) copy-start(bf16[2,32,4,12,128]{4,3,2,1,0:T(8,128)(2,1)} %reshape_squeeze.6) | copy-start | bytes 2359300
  302.5 3.1 copy-start.5
  302.5 3.7 %copy-start.1 = (f32[32,4,16,2,12]{4,2,3,1,0:T(8,128)S(1)}, f32[32,4,16,2,12]{4,2,3,1,0:T(8,128)}, u32[]{:S(2)}) copy-start(f32[32,4,16,2,12]{4,2,3,1,0:T(8,128)} %get-tuple-element.14) | copy-start | bytes 589828
  308.2 1.6 copy-start.2
Sparse Core Ops, SparseCore 0:
  9.5 70.4 all-gather.2
  86.0 215.5 reduce-scatter.1
where the time goes:
time: 320 us
  waiting for transfers between devices  276 us (86%)
  matrix products  16.3 us (5%)
  between operations  13.6 us (4%)
  local copies, waits for them, and re-layouts  9.72 us (3%)
  other arithmetic  3.79 us (1%)
    reduce_scatter x1, waiting for transfers between devices, per_device(): lax.psum_scatter(partial_kv.reshape(step_count, row_count, kv_width), 'te...  204 us
    all_gather x1, waiting for transfers between devices, per_device(): lax.all_gather(new_piece, 'replica', axis=0, tiled=True)  71.5 us
  transfers between devices with their start and end apart: 2, of which 2 were waited for; matrix products, arithmetic and copies ran while one was open for 4% of the time, Pallas kernels for 0%

commit v1 on v0

v1 whole, which is shorter than its diff:
```python
import functools
import math

import jax
import jax.numpy as jnp
from jax import lax
from jax.experimental import pallas as pl
from jax.experimental.pallas import tpu as pltpu
from jax.sharding import PartitionSpec as P

HEAD = 128
QPK = 12
KVH = 4
BLOCK = 16
MASKED = -1e30

def _queries(q_ref, steps, rows, start):
    return jnp.concatenate(
        [q_ref[s*rows+start:s*rows+start+BLOCK, j*HEAD:(j+1)*HEAD] for j in range(QPK) for s in range(steps)], 0)

def _scores(q, k):
    return lax.dot_general(q, k, (((1,), (1,)), ((), ())), preferred_element_type=jnp.float32) * (1.0/math.sqrt(HEAD))

def cache_kernel(q_ref, keys_ref, values_ref, bias_ref, acc_ref, stat_ref, *, steps, rows, slots):
    span = BLOCK*slots
    for half in range(rows//BLOCK):
        q = _queries(q_ref, steps, rows, half*BLOCK)
        n = q.shape[0]
        keys = keys_ref[half*span:(half+1)*span, :]
        values = values_ref[half*span:(half+1)*span, :]
        s = _scores(q, keys).reshape(n//BLOCK, BLOCK, span) + bias_ref[half*BLOCK:(half+1)*BLOCK, :][None]
        s = s.reshape(n, span)
        peak = jnp.max(s, -1, keepdims=True)
        p = jnp.exp(s - peak)
        total = jnp.sum(p, -1, keepdims=True)
        acc_ref[0, half*n:(half+1)*n, :] = jnp.dot(p.astype(jnp.bfloat16), values, preferred_element_type=jnp.float32)
        lane = lax.broadcasted_iota(jnp.int32, (n, HEAD), 1)
        stat_ref[0, half*n:(half+1)*n, :] = jnp.where(lane < HEAD//2, peak, total)

def finish_kernel(q_ref, ksum_ref, vsum_ref, cos_ref, sin_ref, bias_ref, acc_ref, stat_ref, out_ref, *, steps, rows):
    k = jnp.sum(ksum_ref[...].astype(jnp.float32), 0)
    k = (k*cos_ref[...] + pltpu.roll(k, HEAD//2, 1)*sin_ref[...]).astype(jnp.bfloat16)
    v = jnp.sum(vsum_ref[...].astype(jnp.float32), 0).astype(jnp.bfloat16)
    for half in range(rows//BLOCK):
        q = _queries(q_ref, steps, rows, half*BLOCK)
        n = q.shape[0]
        pick = lambda x: jnp.concatenate([x[t*rows+half*BLOCK:t*rows+(half+1)*BLOCK] for t in range(steps)], 0)
        s = _scores(q, pick(k)).reshape(QPK, steps*BLOCK, steps*BLOCK) + bias_ref[...][None]
        s = s.reshape(n, steps*BLOCK)
        stat = stat_ref[0, half*n:(half+1)*n, :]
        old_peak = stat[:, :1]; old_total = stat[:, HEAD//2:HEAD//2+1]
        peak = jnp.maximum(old_peak, jnp.max(s, -1, keepdims=True))
        p = jnp.exp(s - peak)
        keep = jnp.exp(old_peak - peak)
        inv = 1.0 / (old_total*keep + jnp.sum(p, -1, keepdims=True))
        out = acc_ref[0, half*n:(half+1)*n, :]*(keep*inv) + jnp.dot((p*inv).astype(jnp.bfloat16), pick(v), preferred_element_type=jnp.float32)
        out = out.astype(out_ref.dtype)
        for j in range(QPK):
            for t in range(steps):
                at = (j*steps+t)*BLOCK
                out_ref[t*rows+half*BLOCK:t*rows+(half+1)*BLOCK, j*HEAD:(j+1)*HEAD] = out[at:at+BLOCK]

def cache_part(q, kv, lengths):
    steps, rows, width = q.shape
    slots = kv.shape[1]
    wide = QPK*HEAD
    col = jnp.arange(BLOCK*slots, dtype=jnp.int32)[None]
    row = jnp.arange(rows, dtype=jnp.int32)[:, None]
    bias = jnp.where((col//slots == row % BLOCK) & (col % slots < lengths[:, None]), 0.0, MASKED).astype(jnp.float32)
    tall = QPK*steps*rows
    return pl.pallas_call(
        functools.partial(cache_kernel, steps=steps, rows=rows, slots=slots),
        grid=(KVH,),
        in_specs=[pl.BlockSpec((steps*rows, wide), lambda g: (0, g)),
                  pl.BlockSpec((rows*slots, HEAD), lambda g: (0, g)),
                  pl.BlockSpec((rows*slots, HEAD), lambda g: (0, KVH+g)),
                  pl.BlockSpec((rows, BLOCK*slots), lambda g: (0, 0))],
        out_specs=[pl.BlockSpec((1, tall, HEAD), lambda g: (g, 0, 0))]*2,
        out_shape=[jax.ShapeDtypeStruct((KVH, tall, HEAD), jnp.float32)]*2,
        cost_estimate=pl.CostEstimate(flops=4*KVH*tall*BLOCK*slots*HEAD, bytes_accessed=6<<20, transcendentals=KVH*tall*BLOCK*slots),
        compiler_params=pltpu.CompilerParams(vmem_limit_bytes=32<<20),
        name="cache_part",
    )(q.reshape(steps*rows, width), kv.reshape(rows*slots, 2*KVH*HEAD), kv.reshape(rows*slots, 2*KVH*HEAD), bias)

THETA=1000000.0
def tables(lengths, steps):
    positions = (lengths[None, :] + jnp.arange(steps, dtype=jnp.int32)[:, None]).astype(jnp.float32)
    inverse = THETA ** (-(jnp.arange(HEAD//2, dtype=jnp.float32) * 2.0 / HEAD))
    angles = (positions[..., None]*inverse).reshape(-1, HEAD//2)
    c, s = jnp.cos(angles), jnp.sin(angles)
    return jnp.concatenate([c, c], -1), jnp.concatenate([-s, s], -1)

def finish(q, kv_sum, cos, sin, acc, stat):
    steps, rows, width = q.shape
    wide = QPK*HEAD
    tall = acc.shape[1]
    at = jnp.arange(steps*BLOCK, dtype=jnp.int32)
    ok = (at[:, None] % BLOCK == at[None] % BLOCK) & (at[None]//BLOCK <= at[:, None]//BLOCK)
    bias = jnp.where(ok, 0.0, MASKED).astype(jnp.float32)
    n = steps*rows
    pieces = kv_sum.shape[0]
    out = pl.pallas_call(
        functools.partial(finish_kernel, steps=steps, rows=rows),
        grid=(KVH,),
        in_specs=[pl.BlockSpec((n, wide), lambda g: (0, g)),
                  pl.BlockSpec((pieces, n, HEAD), lambda g: (0, 0, g)),
                  pl.BlockSpec((pieces, n, HEAD), lambda g: (0, 0, KVH+g)),
                  pl.BlockSpec((n, HEAD), lambda g: (0, 0)),
                  pl.BlockSpec((n, HEAD), lambda g: (0, 0)),
                  pl.BlockSpec((steps*BLOCK, steps*BLOCK), lambda g: (0, 0)),
                  pl.BlockSpec((1, tall, HEAD), lambda g: (g, 0, 0)),
                  pl.BlockSpec((1, tall, HEAD), lambda g: (g, 0, 0))],
        out_specs=pl.BlockSpec((n, wide), lambda g: (0, g)),
        out_shape=jax.ShapeDtypeStruct((n, width), jnp.bfloat16),
        compiler_params=pltpu.CompilerParams(vmem_limit_bytes=32<<20),
        name="finish",
    )(q.reshape(n, width), kv_sum, kv_sum, cos, sin, bias, acc, stat)
    return out.reshape(steps, rows, width)


def per_device(hidden, queries, kv_cache, lengths, versions, resident, update):
    steps, _, rows, width = hidden.shape
    replicas, shards = lax.axis_size("replica"), lax.axis_size("tensor")
    local = rows // shards
    x = hidden[:, 0].reshape(steps, shards, local, width).transpose(1, 0, 2, 3).reshape(rows*steps, width)
    cores = [[r for r in range(replicas) if r % 2 == c] for c in range(2)]
    mine = lax.all_gather(update[0], "replica", axis=0, axis_index_groups=cores)
    other = lax.ppermute(mine, "replica", [(r, r ^ 1) for r in range(replicas)])
    odd = lax.axis_index("replica") % 2 == 1
    new = jnp.where(odd, jnp.stack([other, mine], 1), jnp.stack([mine, other], 1)).reshape(resident.shape[1:])
    version = lax.dynamic_index_in_dim(versions[:, 0], lax.axis_index("replica"), 0, keepdims=False)
    chosen = jnp.where(version == 1, new, resident[0])
    partial = jnp.dot(x, chosen, preferred_element_type=jnp.float32).astype(jnp.bfloat16)
    pieces = lax.all_to_all(partial.reshape(shards, steps*local, -1), "tensor", 0, 0, tiled=True)
    acc, stat = cache_part(queries[:, 0], kv_cache[0], lengths)
    cos, sin = tables(lengths, steps)
    return finish(queries[:, 0], pieces, cos, sin, acc, stat)[:, None]


def solution(mesh):
    placed = (
        P(None, None, "replica", "tensor"),
        P(None, None, ("replica", "tensor"), None),
        P(None, ("replica", "tensor"), None, None),
        P(("replica", "tensor")),
        P(),
        P(None, "tensor", None),
        P(None, ("tensor", "replica"), None),
    )
    return jax.shard_map(
        per_device,
        mesh=mesh,
        in_specs=placed,
        out_specs=P(None, None, ("replica", "tensor"), None),
        check_vma=False,
    )
```

time: 320 us -> 124 us (0.39)
  the two profiles are of different devices: /device:TPU:8 before, /device:TPU:1 now
where the time goes in v1:
time: 124 us; the launch traced here: 123 us
  waiting for transfers between devices  44 us (35%)
  blocking collectives  32.5 us (26%)
  starting transfers between devices  21.8 us (18%)
  local copies, waits for them, and re-layouts  10.4 us (8%)
  Pallas kernels  9.54 us (8%)
  matrix products  3.79 us (3%)
    all_to_all x1, waiting for transfers between devices, per_device(): lax.all_to_all(partial.reshape(shards, steps * local, -1), 'tensor', 0, 0...  44 us
    all_gather x1, blocking collectives, per_device(): mine = lax.all_gather(update[0], 'replica', axis=0, axis_index_groups=cores)  32.5 us
    all_to_all x1, starting transfers between devices, per_device(): lax.all_to_all(partial.reshape(shards, steps * local, -1), 'tensor', 0, 0...  11.1 us
    ppermute x1, starting transfers between devices, per_device(): other = lax.ppermute(mine, 'replica', [(r, r ^ 1) for r in range(replicas)])  10.8 us
    unnamed x20, local copies, waits for them, and re-layouts  8.65 us
    pallas_call x1, Pallas kernels, finish(): pl.pallas_call(functools.partial(finish_kernel, steps=steps, rows=rows),...  6.93 us
    dot_general x1, matrix products, per_device(): jnp.dot(x, chosen, preferred_element_type=jnp.float32).astype(jnp.bfloat16)  3.79 us
    pallas_call x1, Pallas kernels, cache_part(): pl.pallas_call(functools.partial(cache_kernel, steps=steps, rows=rows, sl...  2.61 us
  transfers between devices with their start and end apart: 2, of which 1 were waited for; matrix products, arithmetic and copies ran while one was open for 2% of the time, Pallas kernels for 2%

profile of v1, /device:TPU:1, one launch (start us, length us, event | category | flops | bytes accessed | tf_op | source)
XLA Modules:
  0.0 123.3 jit_solution(9265521596440593254)
XLA Ops:
  0.0 32.5 %all_gather.3 = bf16[16,24,1024]{2,1,0:T(8,128)(2,1)S(1)} all-gather(bf16[1,24,1024]{2,1,0:T(8,128)(2,1)} %param.13), channel_id=1, replica_groups={{0,32,64,96,128,160,192,224,256,288,320,352,384,416,448,480},{16,48,80,..., dimensions={0}, use_global_device_ids=true | all-gather | bytes 835584 | tf_op jit(solution)/shard_map/all_gather | solution.py:127
  32.5 10.8 %collective-permute-start = (bf16[16,24,1024]{2,1,0:T(8,128)(2,1)S(1)}, bf16[16,24,1024]{2,1,0:T(8,128)(2,1)S(1)}, u32[]{:S(2)}, u32[]{:S(2)}) collective-permute-start(bf16[16,24,1024]{2,1,0:T(8,128)(2,1)S(1)} %all_gather.3), channel_id=1, source_target_pairs={{0,16},{16,0},{32,48},{48,32},{64,80},{80,64},{96,112},{112,96},{1... | collective-permute-start | bytes 2359304 | tf_op jit(solution)/shard_map/ppermute | solution.py:128
  43.3 0.0 copy-start.9
  43.3 1.5 %copy.12 = bf16[16,2,32,768]{3,2,1,0:T(8,128)(2,1)S(1)} copy(bf16[16,2,32,768]{3,2,0,1:T(8,128)(2,1)} %bitcast.28) | data formatting | bytes 3145728 | tf_op jit(solution)/shard_map/transpose | solution.py:125
  44.9 0.6 fusion.6
  45.5 0.1 maximum_select_fusion
  45.6 1.3 %copy-done.8 = bf16[1,768,1024]{2,1,0:T(8,128)(2,1)S(1)} copy-done((bf16[1,768,1024]{2,1,0:T(8,128)(2,1)S(1)}, bf16[1,768,1024]{2,1,0:T(8,128)(2,1)}, u32[]{:S(2)}) %copy-start.8) | copy-done | bytes 1572888
  46.9 3.8 %convolution_convert_fusion = bf16[1024,1024]{0,1:T(8,128)(2,1)} fusion(bf16[1024,768]{1,0:T(8,128)(2,1)S(1)} %bitcast.29, bf16[1,768,1024]{2,1,0:T(8,128)(2,1)S(1)} %bitcast.30, bf16[1,768,1024]{2,1,0:T(8,128)(2,1)S(1)} %copy-done.8, pred[]{:T(512)} %bitcast.1), kind=kOutput, calls=%fused_computation | convolution fusion | flops 1612447744 | bytes 6815745 | tf_op jit(solution)/shard_map/dot_general | solution.py:133
  50.7 11.1 %all-to-all-start = ((bf16[16,64,1024]{2,1,0:T(8,128)(2,1)}), bf16[16,64,1024]{2,1,0:T(8,128)(2,1)S(1)}, u32[]{:S(2)}, u32[]{:S(2)}) async-start(bf16[16,64,1024]{2,1,0:T(8,128)(2,1)} %bitcast.27), calls=%async_computation | async-start | bytes 4194304 | tf_op jit(solution)/shard_map/all_to_all | solution.py:134
  61.8 0.1 add.85
  61.9 0.1 add.87
  62.0 0.1 and_select_fusion.bias_ref
  62.1 1.1 copy-done.1
  63.2 2.6 %cache_part.1 = (f32[4,768,128]{2,1,0:T(8,128)S(1)}, f32[4,768,128]{2,1,0:T(8,128)S(1)}) custom-call(bf16[64,6144]{1,0:T(8,128)(2,1)S(1)} %bitcast.24, bf16[512,1024]{1,0:T(8,128)(2,1)S(1)} %bitcast.22, bf16[512,1024]{1,0:T(8,128)(2,1)S(1)} %bitcast.23, f32[32,256]{1,0:T(8,128)S(1)} %and_select_fusion.bias_ref), custom_call_target="tpu_custom_call" | custom-call | flops 402653184 | bytes 6291456 | tf_op jit(solution)/shard_map/cache_part/pallas_call | solution.py:71
  65.8 1.1 copy-done.3
  67.0 1.2 copy-done.5
  68.1 0.2 fusion.3
  68.3 0.1 pad_maximum_fusion
  68.4 0.1 and_select_fusion.1.bias_ref
  68.5 44.0 %all-to-all-done.ksum_ref.vsum_ref = bf16[16,64,1024]{2,1,0:T(8,128)(2,1)S(1)} async-done(((bf16[16,64,1024]{2,1,0:T(8,128)(2,1)}), bf16[16,64,1024]{2,1,0:T(8,128)(2,1)S(1)}, u32[]{:S(2)}, u32[]{:S(2)}) %all-to-all-start) | async-done | bytes 2097184 | tf_op jit(solution)/shard_map/all_to_all | solution.py:134
  112.5 1.1 copy-done.2
  113.6 1.4 %copy-done.4 = f32[4,768,128]{2,1,0:T(8,128)S(1)} copy-done((f32[4,768,128]{2,1,0:T(8,128)S(1)}, f32[4,768,128]{2,1,0:T(8,128)}, u32[]{:S(2)}) %copy-start.4) | copy-done | bytes 1572888
  115.0 1.4 %copy-done.6 = f32[4,768,128]{2,1,0:T(8,128)S(1)} copy-done((f32[4,768,128]{2,1,0:T(8,128)S(1)}, f32[4,768,128]{2,1,0:T(8,128)}, u32[]{:S(2)}) %copy-start.6) | copy-done | bytes 1572888
  116.4 6.9 %finish.1 = bf16[64,6144]{1,0:T(8,128)(2,1)} custom-call(bf16[64,6144]{1,0:T(8,128)(2,1)S(1)} %bitcast.25, bf16[16,64,1024]{2,1,0:T(8,128)(2,1)S(1)} %all-to-all-done.ksum_ref.vsum_ref, bf16[16,64,1024]{2,1,0:T(8,128)(2,1)S(1)} %all-to-all-done.ksum_ref.vsum_ref, f32[64,128]{1,0:T(8,128)S(1)} %get-tuple-element.12.cos_ref, ...), custom_call_target="tpu_custom_call" | custom-call | tf_op jit(solution)/shard_map/finish/pallas_call | solution.py:102
  (19 shorter events, 0.1 us)
Async XLA Ops:
  32.5 13.0 %collective-permute-start = (bf16[16,24,1024]{2,1,0:T(8,128)(2,1)S(1)}, bf16[16,24,1024]{2,1,0:T(8,128)(2,1)S(1)}, u32[]{:S(2)}, u32[]{:S(2)}) collective-permute-start(bf16[16,24,1024]{2,1,0:T(8,128)(2,1)S(1)} %all_gather.3), channel_id=1, source_target_pairs={{0,16},{16,0},{32,48},{48,32},{64,80},{80,64},{96,112},{112,96},{1... | collective-permute-start | bytes 2359304 | tf_op jit(solution)/shard_map/ppermute | solution.py:128
  43.3 1.6 %copy-start.9 = (s32[32,1]{0,1:T(1,128)S(1)}, s32[32,1]{0,1:T(1,128)}, u32[]{:S(2)}) copy-start(s32[32,1]{0,1:T(1,128)} %param.11) | copy-start | bytes 388
  45.5 1.4 %copy-start.8 = (bf16[1,768,1024]{2,1,0:T(8,128)(2,1)S(1)}, bf16[1,768,1024]{2,1,0:T(8,128)(2,1)}, u32[]{:S(2)}) copy-start(bf16[1,768,1024]{2,1,0:T(8,128)(2,1)} %param.12) | copy-start | bytes 4718596
  50.7 11.1 %copy-start.7 = (s32[32]{0:T(128)S(1)}, s32[32]{0:T(128)}, u32[]{:S(2)}) copy-start(s32[32]{0:T(128)} %param.10) | copy-start | bytes 388
  50.7 11.4 %copy-start = (bf16[1,32,16,1024]{3,2,1,0:T(8,128)(2,1)S(1)}, bf16[1,32,16,1024]{3,2,1,0:T(8,128)(2,1)}, u32[]{:S(2)}) copy-start(bf16[1,32,16,1024]{3,2,1,0:T(8,128)(2,1)} %param.9) | copy-start | bytes 3145732
  50.7 61.8 %all-to-all-start = ((bf16[16,64,1024]{2,1,0:T(8,128)(2,1)}), bf16[16,64,1024]{2,1,0:T(8,128)(2,1)S(1)}, u32[]{:S(2)}, u32[]{:S(2)}) async-start(bf16[16,64,1024]{2,1,0:T(8,128)(2,1)} %bitcast.27), calls=%async_computation | async-start | bytes 4194304 | tf_op jit(solution)/shard_map/all_to_all | solution.py:134
  62.0 1.1 copy-start.1
  65.8 1.2 copy-start.3
  66.9 1.2 copy-start.5
  112.5 1.1 copy-start.2
  113.6 1.4 %copy-start.4 = (f32[4,768,128]{2,1,0:T(8,128)S(1)}, f32[4,768,128]{2,1,0:T(8,128)}, u32[]{:S(2)}) copy-start(f32[4,768,128]{2,1,0:T(8,128)} %copy-done.3) | copy-start | bytes 4718596
  115.0 1.4 %copy-start.6 = (f32[4,768,128]{2,1,0:T(8,128)S(1)}, f32[4,768,128]{2,1,0:T(8,128)}, u32[]{:S(2)}) copy-start(f32[4,768,128]{2,1,0:T(8,128)} %copy-done.5) | copy-start | bytes 4718596

commit v2 on v1

v2 whole, which is shorter than its diff:
```python
import functools
import math

import jax
import jax.numpy as jnp
from jax import lax
from jax.experimental import pallas as pl
from jax.experimental.pallas import tpu as pltpu
from jax.sharding import PartitionSpec as P

HEAD = 128
QPK = 12
KVH = 4
BLOCK = 16
MASKED = -1e30
SCALE = 1.0 / math.sqrt(HEAD)
THETA = 1000000.0
WIDE = QPK * HEAD
YS = 8
ANY = pl.BlockSpec(memory_space=pl.ANY)
VM = pl.BlockSpec(memory_space=pltpu.VMEM)
SM = pl.BlockSpec(memory_space=pltpu.SMEM)
GRANT = 24 << 20

def _queries(q_ref, steps, rows, start, g):
    return jnp.concatenate(
        [q_ref[s*rows+start:s*rows+start+BLOCK, g*WIDE+j*HEAD:g*WIDE+(j+1)*HEAD] for j in range(QPK) for s in range(steps)], 0)

def cache_kernel(q_ref, kv_ref, bias_ref, acc_ref, stat_ref, *, steps, rows, slots):
    span = BLOCK*slots
    n = QPK*steps*BLOCK
    lane = lax.broadcasted_iota(jnp.int32, (n, HEAD), 1)
    stat = jnp.zeros((n, HEAD), jnp.float32)
    for half in range(rows//BLOCK):
        at = slice(half*n, (half+1)*n)
        bias = bias_ref[half*BLOCK:(half+1)*BLOCK, :]
        for g in range(KVH):
            q = _queries(q_ref, steps, rows, half*BLOCK, g)
            keys = kv_ref[half*span:(half+1)*span, g*HEAD:(g+1)*HEAD]
            values = kv_ref[half*span:(half+1)*span, (KVH+g)*HEAD:(KVH+g+1)*HEAD]
            s = lax.dot_general(q, keys, (((1,), (1,)), ((), ())), preferred_element_type=jnp.float32) * SCALE
            s = (s.reshape(n//BLOCK, BLOCK, span) + bias[None]).reshape(n, span)
            peak = jnp.max(s, -1, keepdims=True)
            p = jnp.exp(s - peak).astype(jnp.bfloat16)
            both = jnp.dot(p, jnp.concatenate([values, jnp.ones_like(values)], 1), preferred_element_type=jnp.float32)
            acc_ref[g, at, :] = both[:, :HEAD]
            spot = 2*(half*KVH+g)
            stat = jnp.where(lane == spot, peak, jnp.where(lane == spot+1, both[:, HEAD:], stat))
    stat_ref[...] = stat

def finish_kernel(q_ref, sum_ref, cos_ref, sin_ref, bias_ref, acc_ref, stat_ref, out_ref, held, sems, *, steps, rows):
    copies = []
    pieces = sum_ref.shape[0]
    n = QPK*steps*BLOCK
    for g in range(KVH):
        cols = slice(g*HEAD, (g+1)*HEAD)
        k = sum_ref[0, 0, :, cols].astype(jnp.float32)
        v = sum_ref[0, 1, :, cols].astype(jnp.float32)
        for i in range(1, pieces):
            k = k + sum_ref[i, 0, :, cols].astype(jnp.float32)
            v = v + sum_ref[i, 1, :, cols].astype(jnp.float32)
        k = (k*cos_ref[...] + pltpu.roll(k, HEAD//2, 1)*sin_ref[...]).astype(jnp.bfloat16)
        v = v.astype(jnp.bfloat16)
        v = jnp.concatenate([v, jnp.ones_like(v)], 1)
        for half in range(rows//BLOCK):
            q = _queries(q_ref, steps, rows, half*BLOCK, g)
            pick = lambda x: jnp.concatenate([x[t*rows+half*BLOCK:t*rows+(half+1)*BLOCK] for t in range(steps)], 0)
            s = lax.dot_general(q, pick(k), (((1,), (1,)), ((), ())), preferred_element_type=jnp.float32) * SCALE
            s = (s.reshape(QPK, steps*BLOCK, steps*BLOCK) + bias_ref[...][None]).reshape(n, steps*BLOCK)
            at = slice(half*n, (half+1)*n)
            spot = 2*(half*KVH+g)
            old = jnp.broadcast_to(stat_ref[:, spot:spot+1], (n, HEAD))
            total = jnp.broadcast_to(stat_ref[:, spot+1:spot+2], (n, HEAD))
            peak = jnp.maximum(old, jnp.max(s, -1, keepdims=True))
            p = jnp.exp(s - peak[:, :steps*BLOCK]).astype(jnp.bfloat16)
            both = jnp.dot(p, pick(v), preferred_element_type=jnp.float32)
            keep = jnp.exp(old - peak)
            out = (acc_ref[g, at, :]*keep + both[:, :HEAD]) / (total*keep + both[:, HEAD:])
            out = out.astype(held.dtype)
            for j in range(QPK):
                for t in range(steps):
                    b = (j*steps+t)*BLOCK
                    held[t*rows+half*BLOCK:t*rows+(half+1)*BLOCK, g*WIDE+j*HEAD:g*WIDE+(j+1)*HEAD] = out[b:b+BLOCK]
        part = slice(g*WIDE, (g+1)*WIDE)
        copies.append(pltpu.make_async_copy(held.at[:, part], out_ref.at[:, part], sems.at[g]))
        copies[-1].start()
    for copy in copies:
        copy.wait()

def cache_part(q, kv, lengths):
    steps, rows, width = q.shape
    slots = kv.shape[1]
    col = jnp.arange(BLOCK*slots, dtype=jnp.int32)[None]
    row = jnp.arange(rows, dtype=jnp.int32)[:, None]
    bias = jnp.where((col//slots == row % BLOCK) & (col % slots < lengths[:, None]), 0.0, MASKED).astype(jnp.float32)
    tall = QPK*steps*rows
    return pl.pallas_call(
        functools.partial(cache_kernel, steps=steps, rows=rows, slots=slots),
        in_specs=[VM]*3, out_specs=[VM]*2,
        out_shape=[jax.ShapeDtypeStruct((KVH, tall, HEAD), jnp.float32), jax.ShapeDtypeStruct((QPK*steps*BLOCK, HEAD), jnp.float32)],
        cost_estimate=pl.CostEstimate(flops=4*KVH*tall*BLOCK*slots*HEAD, bytes_accessed=6<<20, transcendentals=KVH*tall*BLOCK*slots),
        compiler_params=pltpu.CompilerParams(vmem_limit_bytes=GRANT),
        name="cache_part",
    )(q.reshape(steps*rows, width), kv.reshape(rows*slots, 2*KVH*HEAD), bias)

def tables(lengths, steps):
    positions = (lengths[None, :] + jnp.arange(steps, dtype=jnp.int32)[:, None]).astype(jnp.float32)
    inverse = THETA ** (-(jnp.arange(HEAD//2, dtype=jnp.float32) * 2.0 / HEAD))
    angles = (positions[..., None]*inverse).reshape(-1, HEAD//2)
    c, s = jnp.cos(angles), jnp.sin(angles)
    return jnp.concatenate([c, c], -1), jnp.concatenate([-s, s], -1)

def finish(q, kv_sum, cos, sin, stats):
    steps, rows, width = q.shape
    at = jnp.arange(steps*BLOCK, dtype=jnp.int32)
    ok = (at[:, None] % BLOCK == at[None] % BLOCK) & (at[None]//BLOCK <= at[:, None]//BLOCK)
    bias = jnp.where(ok, 0.0, MASKED).astype(jnp.float32)
    n = steps*rows
    pieces = kv_sum.shape[0]//2
    out = pl.pallas_call(
        functools.partial(finish_kernel, steps=steps, rows=rows),
        in_specs=[VM]*7, out_specs=ANY,
        scratch_shapes=[pltpu.VMEM((n, width), jnp.bfloat16), pltpu.SemaphoreType.DMA((KVH,))],
        out_shape=jax.ShapeDtypeStruct((n, width), jnp.bfloat16),
        compiler_params=pltpu.CompilerParams(vmem_limit_bytes=GRANT),
        name="finish",
    )(q.reshape(n, width), kv_sum.reshape(pieces, 2, n, KVH*HEAD), cos, sin, bias, *stats)
    return out.reshape(steps, rows, width)

CHUNK = 256


def pieces_kernel(update_ref, out_ref):
    wide = out_ref.shape[2]
    for i in range(out_ref.shape[0]):
        at = (i // 4) * 2 + i % 2
        out_ref[i] = update_ref[:, at * wide : (at + 1) * wide]


def outgoing_kernel(served_ref, x_ref, resident_ref, out_ref, x_held, weight, versions_ref, sems, *, first):
    rows, depth = out_ref.shape
    wide = weight.shape[1]
    chunks = [slice(i, i + CHUNK) for i in range(0, rows, CHUNK)]
    count = len(chunks)
    cols = pl.ds(pl.multiple_of((1 - lax.axis_index("tensor") % 2) * wide, wide), wide)
    load = pltpu.make_async_copy(resident_ref.at[:, cols], weight, sems.at[2 * count])
    arrivals = [pltpu.make_async_copy(x_ref.at[first + c.start : first + c.stop], x_held.at[c], sems.at[n]) for n, c in enumerate(chunks)]
    leaving = [pltpu.make_async_copy(x_held.at[c], out_ref.at[c], sems.at[count + n]) for n, c in enumerate(chunks)]
    short = [pltpu.make_async_copy(x_held.at[c, :wide], out_ref.at[c, :wide], sems.at[count + n]) for n, c in enumerate(chunks)]

    which = pltpu.make_async_copy(served_ref, versions_ref, sems.at[2 * count + 1])
    which.start()
    arrivals[0].start()
    load.start()
    for copy in arrivals[1:]:
        copy.start()
    which.wait()
    fresh = versions_ref[lax.axis_index("replica")] == 1

    @pl.when(fresh)
    def _():
        for n in range(count):
            arrivals[n].wait()
            leaving[n].start()
        load.wait()
        for copy in leaving:
            copy.wait()

    @pl.when(jnp.logical_not(fresh))
    def _():
        load.wait()
        for n, c in enumerate(chunks):
            arrivals[n].wait()
            part = jnp.dot(x_held[c], weight[...], preferred_element_type=jnp.float32)
            x_held[c, :wide] = part.astype(x_held.dtype)
            short[n].start()
        for copy in short:
            copy.wait()


def outgoing(served, x, resident, first, rows):
    depth, wide = x.shape[1], resident.shape[1] // 2
    return pl.pallas_call(
        functools.partial(outgoing_kernel, first=first),
        in_specs=[ANY] * 3,
        out_specs=ANY,
        out_shape=jax.ShapeDtypeStruct((rows, depth), x.dtype),
        scratch_shapes=[
            pltpu.VMEM((rows, depth), x.dtype),
            pltpu.VMEM((depth, wide), x.dtype),
            pltpu.SMEM(served.shape, jnp.int32),
            pltpu.SemaphoreType.DMA((2 * (rows // CHUNK) + 2,)),
        ],
        compiler_params=pltpu.CompilerParams(vmem_limit_bytes=60 << 20),
        name="outgoing",
    )(served, x, resident)


def project_kernel(versions_ref, own_ref, pair_ref, resident_ref, mine_ref, other_ref, out_ref, weight_ref, held, sems):
    depth, wide = own_ref.shape[-1], resident_ref.shape[1] // 2
    steps, shards = own_ref.shape[:2]
    ycount, tall, quarter = mine_ref.shape
    chunk = tall // 4
    high, core = lax.axis_index("tensor") % 2, lax.axis_index("replica") % 2
    fresh = versions_ref[lax.axis_index("replica")] == 1
    blocks = CHUNK // (steps * own_ref.shape[2])

    def rows(ref, i, cols):
        return jnp.concatenate([ref[s, i + b, :, cols] for b in range(blocks) for s in range(steps)], 0)

    def send(i, out):
        held[i : i + blocks] = out.astype(held.dtype).reshape(blocks, -1, wide)
        pltpu.make_async_copy(held.at[i : i + blocks], out_ref.at[i : i + blocks], sems.at[i // blocks]).start()

    @pl.when(fresh)
    def _():
        for got, at in ((mine_ref, core), (other_ref, 1 - core)):
            cols = pl.ds(pl.multiple_of(at * quarter, quarter), quarter)
            for block, source in ((0, high), (1, 1 - high)):
                for low in range(2):
                    take = pl.ds(pl.multiple_of((source * 2 + low) * chunk, chunk), chunk)
                    for y in range(ycount):
                        to = block * depth + (low * ycount + y) * chunk
                        weight_ref[to : to + chunk, cols] = got[y, take, :]
        for i in range(0, shards, blocks):
            out = jnp.dot(rows(own_ref, i, slice(None)), weight_ref[:depth, :], preferred_element_type=jnp.float32)
            send(i, out + jnp.dot(rows(pair_ref, i, slice(None)), weight_ref[depth:, :], preferred_element_type=jnp.float32))

    @pl.when(jnp.logical_not(fresh))
    def _():
        cols = pl.ds(pl.multiple_of(high * wide, wide), wide)
        for i in range(0, shards, blocks):
            out = jnp.dot(rows(own_ref, i, slice(None)), resident_ref[:, cols], preferred_element_type=jnp.float32)
            send(i, out + rows(pair_ref, i, slice(0, wide)).astype(jnp.float32))

    for i in range(0, shards, blocks):
        pltpu.make_async_copy(held.at[i : i + blocks], out_ref.at[i : i + blocks], sems.at[i // blocks]).wait()


def call(kernel, specs, out_specs, out_shape, scratch=(), name=None):
    return pl.pallas_call(
        kernel,
        in_specs=specs,
        out_specs=out_specs,
        out_shape=out_shape,
        scratch_shapes=scratch,
        compiler_params=pltpu.CompilerParams(vmem_limit_bytes=GRANT),
        name=name,
    )


def per_device(hidden, queries, kv_cache, lengths, versions, resident, update):
    steps, _, rows, width = hidden.shape
    replicas, shards = lax.axis_size("replica"), lax.axis_size("tensor")
    both = ("replica", "tensor")
    kind = hidden.dtype
    piece, wide = update.shape[1], update.shape[2] // 2
    served = versions[:, 0]
    groups = [
        [((a * YS + b) * 2 + c) * shards + z * 2 + h for h in range(2) for a in range(2) for c in range(2)]
        for b in range(YS)
        for z in range(shards // 2)
    ]
    lines = [[(a * YS + b) * 2 + c for b in range(YS)] for a in range(2) for c in range(2)]
    pieces = call(pieces_kernel, [pl.BlockSpec()], pl.BlockSpec(), jax.ShapeDtypeStruct((8, piece, wide // 2), kind), name="pieces")(pltpu.with_memory_space_constraint(update[0], pltpu.HBM))
    got = lax.all_to_all(pieces, both, 0, 0, axis_index_groups=groups, tiled=True)
    message = outgoing(served, hidden.reshape(steps * rows, width), resident[0], 0, steps * rows)
    got, message = lax.optimization_barrier((got, message))
    pair = lax.ppermute(message, "tensor", [(i, i ^ 1) for i in range(shards)])
    mine = lax.all_gather(got.reshape(-1, wide // 2), "replica", axis=0, axis_index_groups=lines)
    other = lax.ppermute(mine, "replica", [(i, i ^ 1) for i in range(replicas)])
    local = rows // shards
    partial = pltpu.HBM((shards, steps * local, wide), kind)
    scratch = [pltpu.VMEM((2 * width, wide), kind), pltpu.VMEM(partial.shape, kind), pltpu.SemaphoreType.DMA((steps * rows // CHUNK,))]
    partial = call(project_kernel, [SM] + [VM] * 5, ANY, partial, scratch, "project")(
        served, hidden.reshape(steps, shards, local, width), pair.reshape(steps, shards, local, width), resident[0], mine, other
    )
    summands = lax.all_to_all(partial, "tensor", 0, 0, tiled=True)
    stats = cache_part(queries[:, 0], kv_cache[0], lengths)
    cos, sin = tables(lengths, steps)
    return finish(queries[:, 0], summands, cos, sin, stats)[:, None]


def solution(mesh):
    placed = (
        P(None, None, "replica", "tensor"),
        P(None, None, ("replica", "tensor"), None),
        P(None, ("replica", "tensor"), None, None),
        P(("replica", "tensor")),
        P(),
        P(None, "tensor", None),
        P(None, ("tensor", "replica"), None),
    )
    return jax.shard_map(
        per_device,
        mesh=mesh,
        in_specs=placed,
        out_specs=P(None, None, ("replica", "tensor"), None),
        check_vma=False,
    )
```

time: 124 us -> 99.3 us (0.80)
  the two profiles are of different devices: /device:TPU:1 before, /device:TPU:48 now
where the time goes in v2:
time: 99.3 us; the launch traced here: 98.9 us
  waiting for transfers between devices  35.8 us (36%)
  blocking collectives  27.7 us (28%)
  starting transfers between devices  20.9 us (21%)
  Pallas kernels  11.2 us (11%)
  local copies, waits for them, and re-layouts  2.7 us (3%)
    all_gather x1, blocking collectives, per_device(): lax.all_gather(got.reshape(-1, wide // 2), 'replica', axis=0, axis_index_...  27.7 us
    all_to_all x1, waiting for transfers between devices, per_device(): summands = lax.all_to_all(partial, 'tensor', 0, 0, tiled=True)  25.5 us
    all_to_all x1, starting transfers between devices, per_device(): summands = lax.all_to_all(partial, 'tensor', 0, 0, tiled=True)  11.9 us
    ppermute x1, waiting for transfers between devices, per_device(): pair = lax.ppermute(message, 'tensor', [(i, i ^ 1) for i in range(shards)])  4.95 us
    all_to_all x1, starting transfers between devices, per_device(): lax.all_to_all(pieces, both, 0, 0, axis_index_groups=groups, tiled=True)  4.3 us
    pallas_call x1, Pallas kernels, per_device(): call(project_kernel, [SM] + [VM] * 5, ANY, partial, scratch, 'project')  3.24 us
    all_to_all x1, waiting for transfers between devices, per_device(): lax.all_to_all(pieces, both, 0, 0, axis_index_groups=groups, tiled=True)  3.13 us
    ppermute x1, starting transfers between devices, per_device(): pair = lax.ppermute(message, 'tensor', [(i, i ^ 1) for i in range(shards)])  2.8 us
  transfers between devices with their start and end apart: 4, of which 4 were waited for; matrix products, arithmetic and copies ran while one was open for 1% of the time, Pallas kernels for 4%

profile of v2, /device:TPU:48, one launch (start us, length us, event | category | flops | bytes accessed | tf_op | source)
XLA Modules:
  0.0 98.9 jit_solution(18420880343456007442)
XLA Ops:
  0.0 1.4 %pieces.1 = bf16[8,24,256]{2,1,0:T(8,128)(2,1)} custom-call(bf16[24,1024]{1,0:T(8,128)(2,1)} %bitcast.27), custom_call_target="tpu_custom_call" | custom-call | tf_op jit(solution)/shard_map/pieces/pallas_call | solution.py:265
  1.4 4.3 %all-to-all-start = ((bf16[8,24,256]{2,1,0:T(8,128)(2,1)}), bf16[8,24,256]{2,1,0:T(8,128)(2,1)S(1)}, u32[]{:S(2)}, u32[]{:S(2)}) async-start(bf16[8,24,256]{2,1,0:T(8,128)(2,1)} %pieces.1), calls=%async_computation | async-start | bytes 196608 | tf_op jit(solution)/shard_map/all_to_all | solution.py:266
  5.8 0.0 copy-start.1
  5.8 2.6 %outgoing.1 = bf16[1024,768]{1,0:T(8,128)(2,1)} custom-call(s32[32]{0:T(128)} %bitcast.24, bf16[1024,768]{1,0:T(8,128)(2,1)} %bitcast.15, bf16[768,1024]{1,0:T(8,128)(2,1)} %bitcast.17), custom_call_target="tpu_custom_call" | custom-call | tf_op jit(solution)/shard_map/outgoing/pallas_call | solution.py:183
  8.4 3.1 %all-to-all-done = bf16[8,24,256]{2,1,0:T(8,128)(2,1)S(1)} async-done(((bf16[8,24,256]{2,1,0:T(8,128)(2,1)}), bf16[8,24,256]{2,1,0:T(8,128)(2,1)S(1)}, u32[]{:S(2)}, u32[]{:S(2)}) %all-to-all-start) | async-done | bytes 98336 | tf_op jit(solution)/shard_map/all_to_all | solution.py:266
  11.5 2.8 %collective-permute-start = (bf16[1024,768]{1,0:T(8,128)(2,1)}, bf16[1024,768]{1,0:T(8,128)(2,1)S(1)}, u32[]{:S(2)}, u32[]{:S(2)}) collective-permute-start(bf16[1024,768]{1,0:T(8,128)(2,1)} %outgoing.1), channel_id=1, source_target_pairs={{0,1},{1,0},{2,3},{3,2},{4,5},{5,4},{6,7},{7,6},{8,9},{9,8},{10,11... | collective-permute-start | bytes 4718600 | tf_op jit(solution)/shard_map/ppermute | solution.py:269
  14.4 27.7 %all_gather.3.mine_ref = bf16[8,192,256]{2,1,0:T(8,128)(2,1)S(1)} all-gather(bf16[1,192,256]{2,1,0:T(8,128)(2,1)S(1)} %bitcast.26), channel_id=1, replica_groups={{0,32,64,96,128,160,192,224},{16,48,80,112,144,176,208,240},{256,288,32..., dimensions={0}, use_global_device_ids=true | all-gather | bytes 884736 | tf_op jit(solution)/shard_map/all_gather | solution.py:270
  42.0 1.9 %collective-permute-start.1 = (bf16[8,192,256]{2,1,0:T(8,128)(2,1)S(1)}, bf16[8,192,256]{2,1,0:T(8,128)(2,1)S(1)}, u32[]{:S(2)}, u32[]{:S(2)}) collective-permute-start(bf16[8,192,256]{2,1,0:T(8,128)(2,1)S(1)} %all_gather.3.mine_ref), channel_id=1, source_target_pairs={{0,16},{16,0},{32,48},{48,32},{64,80},{80,64},{96,112},{112,96},{1... | collective-permute-start | bytes 2359304 | tf_op jit(solution)/shard_map/ppermute | solution.py:271
  43.9 2.3 %collective-permute-done.1.other_ref = bf16[8,192,256]{2,1,0:T(8,128)(2,1)S(1)} collective-permute-done((bf16[8,192,256]{2,1,0:T(8,128)(2,1)S(1)}, bf16[8,192,256]{2,1,0:T(8,128)(2,1)S(1)}, u32[]{:S(2)}, u32[]{:S(2)}) %collective-permute-start.1) | collective-permute-done | bytes 786464 | tf_op jit(solution)/shard_map/ppermute | solution.py:271
  46.2 5.0 %collective-permute-done = bf16[1024,768]{1,0:T(8,128)(2,1)S(1)} collective-permute-done((bf16[1024,768]{1,0:T(8,128)(2,1)}, bf16[1024,768]{1,0:T(8,128)(2,1)S(1)}, u32[]{:S(2)}, u32[]{:S(2)}) %collective-permute-start) | collective-permute-done | bytes 1572896 | tf_op jit(solution)/shard_map/ppermute | solution.py:269
  51.1 3.2 %project.1 = bf16[16,64,512]{2,1,0:T(8,128)(2,1)} custom-call(s32[32]{0:T(128)S(1)} %bitcast.25, bf16[2,16,32,768]{3,2,1,0:T(8,128)(2,1)S(1)} %bitcast.16, bf16[2,16,32,768]{3,2,1,0:T(8,128)(2,1)S(1)} %bitcast.22, bf16[768,1024]{1,0:T(8,128)(2,1)S(1)} %bitcast.18, bf16[8,192,256]{2,1,0:T(8,128)(2,1)S(1)} %all_gather.3.mine_ref, ...), custom_call_target="tpu_custom_call" | custom-call | tf_op jit(solution)/shard_map/project/pallas_call | solution.py:275
  54.4 11.9 %all-to-all-start.1 = ((bf16[16,64,512]{2,1,0:T(8,128)(2,1)}), bf16[16,64,512]{2,1,0:T(8,128)(2,1)S(1)}, u32[]{:S(2)}, u32[]{:S(2)}) async-start(bf16[16,64,512]{2,1,0:T(8,128)(2,1)} %project.1), calls=%async_computation.1 | async-start | bytes 2097152 | tf_op jit(solution)/shard_map/all_to_all | solution.py:278
  66.4 0.1 add.75
  66.5 0.1 add.77
  66.5 0.1 and_select_fusion.bias_ref
  66.6 1.2 %copy-done.3 = bf16[1,32,16,1024]{3,2,1,0:T(8,128)(2,1)S(1)} copy-done((bf16[1,32,16,1024]{3,2,1,0:T(8,128)(2,1)S(1)}, bf16[1,32,16,1024]{3,2,1,0:T(8,128)(2,1)}, u32[]{:S(2)}) %copy-start.3) | copy-done | bytes 1048600
  67.9 1.2 %cache_part.1 = (f32[4,768,128]{2,1,0:T(8,128)S(1)}, f32[384,128]{1,0:T(8,128)S(1)}) custom-call(bf16[64,6144]{1,0:T(8,128)(2,1)S(1)} %bitcast.20, bf16[512,1024]{1,0:T(8,128)(2,1)S(1)} %bitcast.23, f32[32,256]{1,0:T(8,128)S(1)} %and_select_fusion.bias_ref), custom_call_target="tpu_custom_call" | custom-call | flops 402653184 | bytes 6291456 | tf_op jit(solution)/shard_map/cache_part/pallas_call | solution.py:97
  69.1 0.2 fusion
  69.3 0.1 pad_maximum_fusion
  69.4 0.3 copy-done.4
  69.7 0.1 and_select_fusion.1.bias_ref
  69.8 25.5 %all-to-all-done.1 = bf16[16,64,512]{2,1,0:T(8,128)(2,1)S(1)} async-done(((bf16[16,64,512]{2,1,0:T(8,128)(2,1)}), bf16[16,64,512]{2,1,0:T(8,128)(2,1)S(1)}, u32[]{:S(2)}, u32[]{:S(2)}) %all-to-all-start.1) | async-done | bytes 1048608 | tf_op jit(solution)/shard_map/all_to_all | solution.py:278
  95.3 0.9 copy-done.5
  96.2 2.7 %finish.1 = bf16[64,6144]{1,0:T(8,128)(2,1)} custom-call(bf16[64,6144]{1,0:T(8,128)(2,1)S(1)} %bitcast.21, bf16[8,2,64,512]{3,2,1,0:T(8,128)(2,1)S(1)} %bitcast.19, f32[64,128]{1,0:T(8,128)S(1)} %get-tuple-element.16.cos_ref, f32[64,128]{1,0:T(8,128)S(1)} %get-tuple-element.17.sin_ref, f32[32,32]{1,0:T(8,128)S(1)} %and_select_fusion.1.bias_ref, ...), custom_call_target="tpu_custom_call" | custom-call | tf_op jit(solution)/shard_map/finish/pallas_call | solution.py:120
  (18 shorter events, 0.1 us)
Async XLA Ops:
  1.4 10.1 %all-to-all-start = ((bf16[8,24,256]{2,1,0:T(8,128)(2,1)}), bf16[8,24,256]{2,1,0:T(8,128)(2,1)S(1)}, u32[]{:S(2)}, u32[]{:S(2)}) async-start(bf16[8,24,256]{2,1,0:T(8,128)(2,1)} %pieces.1), calls=%async_computation | async-start | bytes 196608 | tf_op jit(solution)/shard_map/all_to_all | solution.py:266
  5.7 45.4 %copy-start = (bf16[2,1,512,768]{3,2,1,0:T(8,128)(2,1)S(1)}, bf16[2,1,512,768]{3,2,1,0:T(8,128)(2,1)}, u32[]{:S(2)}) copy-start(bf16[2,1,512,768]{3,2,1,0:T(8,128)(2,1)} %param.7) | copy-start | bytes 4718596
  5.8 45.4 %copy-start.1 = (bf16[1,768,1024]{2,1,0:T(8,128)(2,1)S(1)}, bf16[1,768,1024]{2,1,0:T(8,128)(2,1)}, u32[]{:S(2)}) copy-start(bf16[1,768,1024]{2,1,0:T(8,128)(2,1)} %param.12) | copy-start | bytes 4718596
  5.8 45.4 %copy-start.6 = (s32[32,1]{0,1:T(1,128)S(1)}, s32[32,1]{0,1:T(1,128)}, u32[]{:S(2)}) copy-start(s32[32,1]{0,1:T(1,128)} %param.11) | copy-start | bytes 388
  11.5 39.6 %collective-permute-start = (bf16[1024,768]{1,0:T(8,128)(2,1)}, bf16[1024,768]{1,0:T(8,128)(2,1)S(1)}, u32[]{:S(2)}, u32[]{:S(2)}) collective-permute-start(bf16[1024,768]{1,0:T(8,128)(2,1)} %outgoing.1), channel_id=1, source_target_pairs={{0,1},{1,0},{2,3},{3,2},{4,5},{5,4},{6,7},{7,6},{8,9},{9,8},{10,11... | collective-permute-start | bytes 4718600 | tf_op jit(solution)/shard_map/ppermute | solution.py:269
  42.0 4.2 %collective-permute-start.1 = (bf16[8,192,256]{2,1,0:T(8,128)(2,1)S(1)}, bf16[8,192,256]{2,1,0:T(8,128)(2,1)S(1)}, u32[]{:S(2)}, u32[]{:S(2)}) collective-permute-start(bf16[8,192,256]{2,1,0:T(8,128)(2,1)S(1)} %all_gather.3.mine_ref), channel_id=1, source_target_pairs={{0,16},{16,0},{32,48},{48,32},{64,80},{80,64},{96,112},{112,96},{1... | collective-permute-start | bytes 2359304 | tf_op jit(solution)/shard_map/ppermute | solution.py:271
  54.4 12.0 %copy-start.7 = (s32[32]{0:T(128)S(1)}, s32[32]{0:T(128)}, u32[]{:S(2)}) copy-start(s32[32]{0:T(128)} %param.10) | copy-start | bytes 388
  54.4 12.2 %copy-start.2 = (bf16[2,1,32,6144]{3,2,1,0:T(8,128)(2,1)S(1)}, bf16[2,1,32,6144]{3,2,1,0:T(8,128)(2,1)}, u32[]{:S(2)}) copy-start(bf16[2,1,32,6144]{3,2,1,0:T(8,128)(2,1)} %param.8) | copy-start | bytes 2359300
  54.4 40.9 %all-to-all-start.1 = ((bf16[16,64,512]{2,1,0:T(8,128)(2,1)}), bf16[16,64,512]{2,1,0:T(8,128)(2,1)S(1)}, u32[]{:S(2)}, u32[]{:S(2)}) async-start(bf16[16,64,512]{2,1,0:T(8,128)(2,1)} %project.1), calls=%async_computation.1 | async-start | bytes 2097152 | tf_op jit(solution)/shard_map/all_to_all | solution.py:278
  66.6 1.2 %copy-start.3 = (bf16[1,32,16,1024]{3,2,1,0:T(8,128)(2,1)S(1)}, bf16[1,32,16,1024]{3,2,1,0:T(8,128)(2,1)}, u32[]{:S(2)}) copy-start(bf16[1,32,16,1024]{3,2,1,0:T(8,128)(2,1)} %param.9) | copy-start | bytes 3145732
  69.1 0.7 copy-start.4
  95.3 0.9 copy-start.5

commit v3 on v2

--- a/solution.py
+++ b/solution.py
@@ -26,10 +26,12 @@
     return jnp.concatenate(
         [q_ref[s*rows+start:s*rows+start+BLOCK, g*WIDE+j*HEAD:g*WIDE+(j+1)*HEAD] for j in range(QPK) for s in range(steps)], 0)
 
-def cache_kernel(q_ref, kv_ref, bias_ref, acc_ref, stat_ref, *, steps, rows, slots):
+def cache_kernel(q_ref, kv_ref, bias_ref, acc_ref, *, steps, rows, slots):
     span = BLOCK*slots
     n = QPK*steps*BLOCK
     lane = lax.broadcasted_iota(jnp.int32, (n, HEAD), 1)
+    tall = QPK*steps*rows
+    spots = 2*KVH*(rows//BLOCK)
     stat = jnp.zeros((n, HEAD), jnp.float32)
     for half in range(rows//BLOCK):
         at = slice(half*n, (half+1)*n)
@@ -43,15 +45,20 @@
             peak = jnp.max(s, -1, keepdims=True)
             p = jnp.exp(s - peak).astype(jnp.bfloat16)
             both = jnp.dot(p, jnp.concatenate([values, jnp.ones_like(values)], 1), preferred_element_type=jnp.float32)
-            acc_ref[g, at, :] = both[:, :HEAD]
+            acc_ref[g*tall+half*n:g*tall+(half+1)*n, :] = both[:, :HEAD]
             spot = 2*(half*KVH+g)
             stat = jnp.where(lane == spot, peak, jnp.where(lane == spot+1, both[:, HEAD:], stat))
-    stat_ref[...] = stat
-
-def finish_kernel(q_ref, sum_ref, cos_ref, sin_ref, bias_ref, acc_ref, stat_ref, out_ref, held, sems, *, steps, rows):
+    turned = stat.T
+    for k in range(n//HEAD):
+        acc_ref[KVH*tall+k*spots:KVH*tall+(k+1)*spots, :] = turned[:spots, k*HEAD:(k+1)*HEAD]
+
+def finish_kernel(q_ref, sum_ref, cos_ref, sin_ref, bias_ref, acc_ref, out_ref, held, sems, *, steps, rows):
     copies = []
     pieces = sum_ref.shape[0]
     n = QPK*steps*BLOCK
+    tall = QPK*steps*rows
+    spots = 2*KVH*(rows//BLOCK)
+    stat = jnp.concatenate([acc_ref[KVH*tall+k*spots:KVH*tall+(k+1)*spots, :] for k in range(n//HEAD)], 1).T
     for g in range(KVH):
         cols = slice(g*HEAD, (g+1)*HEAD)
         k = sum_ref[0, 0, :, cols].astype(jnp.float32)
@@ -69,13 +76,13 @@
             s = (s.reshape(QPK, steps*BLOCK, steps*BLOCK) + bias_ref[...][None]).reshape(n, steps*BLOCK)
             at = slice(half*n, (half+1)*n)
             spot = 2*(half*KVH+g)
-            old = jnp.broadcast_to(stat_ref[:, spot:spot+1], (n, HEAD))
-            total = jnp.broadcast_to(stat_ref[:, spot+1:spot+2], (n, HEAD))
+            old = jnp.broadcast_to(stat[:, spot:spot+1], (n, HEAD))
+            total = jnp.broadcast_to(stat[:, spot+1:spot+2], (n, HEAD))
             peak = jnp.maximum(old, jnp.max(s, -1, keepdims=True))
             p = jnp.exp(s - peak[:, :steps*BLOCK]).astype(jnp.bfloat16)
             both = jnp.dot(p, pick(v), preferred_element_type=jnp.float32)
             keep = jnp.exp(old - peak)
-            out = (acc_ref[g, at, :]*keep + both[:, :HEAD]) / (total*keep + both[:, HEAD:])
+            out = (acc_ref[g*tall+half*n:g*tall+(half+1)*n, :]*keep + both[:, :HEAD]) / (total*keep + both[:, HEAD:])
             out = out.astype(held.dtype)
             for j in range(QPK):
                 for t in range(steps):
@@ -96,8 +103,8 @@
     tall = QPK*steps*rows
     return pl.pallas_call(
         functools.partial(cache_kernel, steps=steps, rows=rows, slots=slots),
-        in_specs=[VM]*3, out_specs=[VM]*2,
-        out_shape=[jax.ShapeDtypeStruct((KVH, tall, HEAD), jnp.float32), jax.ShapeDtypeStruct((QPK*steps*BLOCK, HEAD), jnp.float32)],
+        in_specs=[VM]*3, out_specs=VM,
+        out_shape=jax.ShapeDtypeStruct((KVH*tall + 2*KVH*(rows//BLOCK)*(QPK*steps*BLOCK//HEAD), HEAD), jnp.float32),
         cost_estimate=pl.CostEstimate(flops=4*KVH*tall*BLOCK*slots*HEAD, bytes_accessed=6<<20, transcendentals=KVH*tall*BLOCK*slots),
         compiler_params=pltpu.CompilerParams(vmem_limit_bytes=GRANT),
         name="cache_part",
@@ -119,12 +126,12 @@
     pieces = kv_sum.shape[0]//2
     out = pl.pallas_call(
         functools.partial(finish_kernel, steps=steps, rows=rows),
-        in_specs=[VM]*7, out_specs=ANY,
+        in_specs=[VM]*6, out_specs=ANY,
         scratch_shapes=[pltpu.VMEM((n, width), jnp.bfloat16), pltpu.SemaphoreType.DMA((KVH,))],
         out_shape=jax.ShapeDtypeStruct((n, width), jnp.bfloat16),
         compiler_params=pltpu.CompilerParams(vmem_limit_bytes=GRANT),
         name="finish",
-    )(q.reshape(n, width), kv_sum.reshape(pieces, 2, n, KVH*HEAD), cos, sin, bias, *stats)
+    )(q.reshape(n, width), kv_sum.reshape(pieces, 2, n, KVH*HEAD), cos, sin, bias, stats)
     return out.reshape(steps, rows, width)
 
 CHUNK = 256
@@ -196,8 +203,8 @@
     )(served, x, resident)
 
 
-def project_kernel(versions_ref, own_ref, pair_ref, resident_ref, mine_ref, other_ref, out_ref, weight_ref, held, sems):
-    depth, wide = own_ref.shape[-1], resident_ref.shape[1] // 2
+def own_kernel(versions_ref, own_ref, resident_ref, mine_ref, other_ref, part_ref, far_ref, near):
+    depth, wide = far_ref.shape
     steps, shards = own_ref.shape[:2]
     ycount, tall, quarter = mine_ref.shape
     chunk = tall // 4
@@ -205,33 +212,51 @@
     fresh = versions_ref[lax.axis_index("replica")] == 1
     blocks = CHUNK // (steps * own_ref.shape[2])
 
-    def rows(ref, i, cols):
-        return jnp.concatenate([ref[s, i + b, :, cols] for b in range(blocks) for s in range(steps)], 0)
-
-    def send(i, out):
-        held[i : i + blocks] = out.astype(held.dtype).reshape(blocks, -1, wide)
-        pltpu.make_async_copy(held.at[i : i + blocks], out_ref.at[i : i + blocks], sems.at[i // blocks]).start()
+    def run(weight):
+        for i in range(0, shards, blocks):
+            rows = jnp.concatenate([own_ref[s, i + b] for b in range(blocks) for s in range(steps)], 0)
+            part_ref[i * CHUNK // blocks : (i + blocks) * CHUNK // blocks] = jnp.dot(rows, weight, preferred_element_type=jnp.float32)
 
     @pl.when(fresh)
     def _():
         for got, at in ((mine_ref, core), (other_ref, 1 - core)):
             cols = pl.ds(pl.multiple_of(at * quarter, quarter), quarter)
-            for block, source in ((0, high), (1, 1 - high)):
+            for into, source in ((near, high), (far_ref, 1 - high)):
                 for low in range(2):
                     take = pl.ds(pl.multiple_of((source * 2 + low) * chunk, chunk), chunk)
                     for y in range(ycount):
-                        to = block * depth + (low * ycount + y) * chunk
-                        weight_ref[to : to + chunk, cols] = got[y, take, :]
+                        to = (low * ycount + y) * chunk
+                        into[to : to + chunk, cols] = got[y, take, :]
+        run(near[...])
+
+    @pl.when(jnp.logical_not(fresh))
+    def _():
+        run(resident_ref[:, pl.ds(pl.multiple_of(high * wide, wide), wide)])
+
+
+def pair_kernel(versions_ref, part_ref, far_ref, pair_ref, out_ref, held, sems):
+    wide = far_ref.shape[1]
+    steps, shards = pair_ref.shape[:2]
+    fresh = versions_ref[lax.axis_index("replica")] == 1
+    blocks = CHUNK // (steps * pair_ref.shape[2])
+
+    def rows(i, cols):
+        return jnp.concatenate([pair_ref[s, i + b, :, cols] for b in range(blocks) for s in range(steps)], 0)
+
+    def send(i, out):
+        out = out + part_ref[i * CHUNK // blocks : (i + blocks) * CHUNK // blocks]
+        held[i : i + blocks] = out.astype(held.dtype).reshape(blocks, -1, wide)
+        pltpu.make_async_copy(held.at[i : i + blocks], out_ref.at[i : i + blocks], sems.at[i // blocks]).start()
+
+    @pl.when(fresh)
+    def _():
         for i in range(0, shards, blocks):
-            out = jnp.dot(rows(own_ref, i, slice(None)), weight_ref[:depth, :], preferred_element_type=jnp.float32)
-            send(i, out + jnp.dot(rows(pair_ref, i, slice(None)), weight_ref[depth:, :], preferred_element_type=jnp.float32))
+            send(i, jnp.dot(rows(i, slice(None)), far_ref[...], preferred_element_type=jnp.float32))
 
     @pl.when(jnp.logical_not(fresh))
     def _():
-        cols = pl.ds(pl.multiple_of(high * wide, wide), wide)
         for i in range(0, shards, blocks):
-            out = jnp.dot(rows(own_ref, i, slice(None)), resident_ref[:, cols], preferred_element_type=jnp.float32)
-            send(i, out + rows(pair_ref, i, slice(0, wide)).astype(jnp.float32))
+            send(i, rows(i, slice(0, wide)).astype(jnp.float32))
 
     for i in range(0, shards, blocks):
         pltpu.make_async_copy(held.at[i : i + blocks], out_ref.at[i : i + blocks], sems.at[i // blocks]).wait()
@@ -270,10 +295,14 @@
     mine = lax.all_gather(got.reshape(-1, wide // 2), "replica", axis=0, axis_index_groups=lines)
     other = lax.ppermute(mine, "replica", [(i, i ^ 1) for i in range(replicas)])
     local = rows // shards
-    partial = pltpu.HBM((shards, steps * local, wide), kind)
-    scratch = [pltpu.VMEM((2 * width, wide), kind), pltpu.VMEM(partial.shape, kind), pltpu.SemaphoreType.DMA((steps * rows // CHUNK,))]
-    partial = call(project_kernel, [SM] + [VM] * 5, ANY, partial, scratch, "project")(
-        served, hidden.reshape(steps, shards, local, width), pair.reshape(steps, shards, local, width), resident[0], mine, other
+    shape = (shards, steps * local, wide)
+    part = [jax.ShapeDtypeStruct((steps * rows, wide), jnp.float32), jax.ShapeDtypeStruct((width, wide), kind)]
+    part, far = call(own_kernel, [SM] + [VM] * 4, [VM] * 2, part, [pltpu.VMEM((width, wide), kind)], "own")(
+        served, hidden.reshape(steps, shards, local, width), resident[0], mine, other
+    )
+    scratch = [pltpu.VMEM(shape, kind), pltpu.SemaphoreType.DMA((steps * rows // CHUNK,))]
+    partial = call(pair_kernel, [SM] + [VM] * 3, ANY, pltpu.HBM(shape, kind), scratch, "pair")(
+        served, part, far, pair.reshape(steps, shards, local, width)
     )
     summands = lax.all_to_all(partial, "tensor", 0, 0, tiled=True)
     stats = cache_part(queries[:, 0], kv_cache[0], lengths)

time: 99.3 us -> 97.8 us (0.985)
  the two profiles are of different devices: /device:TPU:48 before, /device:TPU:32 now
where the time goes in v3:
time: 97.8 us; the launch traced here: 97.4 us
  waiting for transfers between devices  36.3 us (37%)
  blocking collectives  26.1 us (27%)
  starting transfers between devices  20.9 us (21%)
  Pallas kernels  12.1 us (12%)
  local copies, waits for them, and re-layouts  1.42 us (1%)
    all_gather x1, blocking collectives, per_device(): lax.all_gather(got.reshape(-1, wide // 2), 'replica', axis=0, axis_index_...  26.1 us
    all_to_all x1, waiting for transfers between devices, per_device(): summands = lax.all_to_all(partial, 'tensor', 0, 0, tiled=True)  26 us
    all_to_all x1, starting transfers between devices, per_device(): summands = lax.all_to_all(partial, 'tensor', 0, 0, tiled=True)  11.9 us
    ppermute x1, waiting for transfers between devices, per_device(): pair = lax.ppermute(message, 'tensor', [(i, i ^ 1) for i in range(shards)])  4.88 us
    all_to_all x1, starting transfers between devices, per_device(): lax.all_to_all(pieces, both, 0, 0, axis_index_groups=groups, tiled=True)  4.3 us
    all_to_all x1, waiting for transfers between devices, per_device(): lax.all_to_all(pieces, both, 0, 0, axis_index_groups=groups, tiled=True)  3.13 us
    pallas_call x1, Pallas kernels, finish(): pl.pallas_call(functools.partial(finish_kernel, steps=steps, rows=rows),...  2.9 us
    ppermute x1, starting transfers between devices, per_device(): pair = lax.ppermute(message, 'tensor', [(i, i ^ 1) for i in range(shards)])  2.8 us
  transfers between devices with their start and end apart: 4, of which 4 were waited for; matrix products, arithmetic and copies ran while one was open for 1% of the time, Pallas kernels for 6%

profile of v3, /device:TPU:32, one launch (start us, length us, event | category | flops | bytes accessed | tf_op | source)
XLA Modules:
  0.0 97.4 jit_solution(663531544167609816)
XLA Ops:
  0.0 1.4 %pieces.1 = bf16[8,24,256]{2,1,0:T(8,128)(2,1)} custom-call(bf16[24,1024]{1,0:T(8,128)(2,1)} %bitcast.28), custom_call_target="tpu_custom_call" | custom-call | tf_op jit(solution)/shard_map/pieces/pallas_call | solution.py:290
  1.4 4.3 %all-to-all-start = ((bf16[8,24,256]{2,1,0:T(8,128)(2,1)}), bf16[8,24,256]{2,1,0:T(8,128)(2,1)S(1)}, u32[]{:S(2)}, u32[]{:S(2)}) async-start(bf16[8,24,256]{2,1,0:T(8,128)(2,1)} %pieces.1), calls=%async_computation | async-start | bytes 196608 | tf_op jit(solution)/shard_map/all_to_all | solution.py:291
  5.8 0.0 copy-start.1
  5.8 0.0 copy-start.4
  5.8 2.6 %outgoing.1 = bf16[1024,768]{1,0:T(8,128)(2,1)} custom-call(s32[32]{0:T(128)} %bitcast.24, bf16[1024,768]{1,0:T(8,128)(2,1)} %bitcast.15, bf16[768,1024]{1,0:T(8,128)(2,1)} %bitcast.17), custom_call_target="tpu_custom_call" | custom-call | tf_op jit(solution)/shard_map/outgoing/pallas_call | solution.py:190
  8.4 3.1 %all-to-all-done = bf16[8,24,256]{2,1,0:T(8,128)(2,1)S(1)} async-done(((bf16[8,24,256]{2,1,0:T(8,128)(2,1)}), bf16[8,24,256]{2,1,0:T(8,128)(2,1)S(1)}, u32[]{:S(2)}, u32[]{:S(2)}) %all-to-all-start) | async-done | bytes 98336 | tf_op jit(solution)/shard_map/all_to_all | solution.py:291
  11.5 2.8 %collective-permute-start.1 = (bf16[1024,768]{1,0:T(8,128)(2,1)}, bf16[1024,768]{1,0:T(8,128)(2,1)S(1)}, u32[]{:S(2)}, u32[]{:S(2)}) collective-permute-start(bf16[1024,768]{1,0:T(8,128)(2,1)} %outgoing.1), channel_id=1, source_target_pairs={{0,1},{1,0},{2,3},{3,2},{4,5},{5,4},{6,7},{7,6},{8,9},{9,8},{10,11... | collective-permute-start | bytes 4718600 | tf_op jit(solution)/shard_map/ppermute | solution.py:294
  14.4 26.1 %all_gather.3.mine_ref = bf16[8,192,256]{2,1,0:T(8,128)(2,1)S(1)} all-gather(bf16[1,192,256]{2,1,0:T(8,128)(2,1)S(1)} %bitcast.27), channel_id=1, replica_groups={{0,32,64,96,128,160,192,224},{16,48,80,112,144,176,208,240},{256,288,32..., dimensions={0}, use_global_device_ids=true | all-gather | bytes 884736 | tf_op jit(solution)/shard_map/all_gather | solution.py:295
  40.4 1.9 %collective-permute-start = (bf16[8,192,256]{2,1,0:T(8,128)(2,1)S(1)}, bf16[8,192,256]{2,1,0:T(8,128)(2,1)S(1)}, u32[]{:S(2)}, u32[]{:S(2)}) collective-permute-start(bf16[8,192,256]{2,1,0:T(8,128)(2,1)S(1)} %all_gather.3.mine_ref), channel_id=1, source_target_pairs={{0,16},{16,0},{32,48},{48,32},{64,80},{80,64},{96,112},{112,96},{1... | collective-permute-start | bytes 2359304 | tf_op jit(solution)/shard_map/ppermute | solution.py:296
  42.3 2.3 %collective-permute-done.other_ref = bf16[8,192,256]{2,1,0:T(8,128)(2,1)S(1)} collective-permute-done((bf16[8,192,256]{2,1,0:T(8,128)(2,1)S(1)}, bf16[8,192,256]{2,1,0:T(8,128)(2,1)S(1)}, u32[]{:S(2)}, u32[]{:S(2)}) %collective-permute-start) | collective-permute-done | bytes 786464 | tf_op jit(solution)/shard_map/ppermute | solution.py:296
  44.6 1.6 %own.1 = (f32[1024,512]{1,0:T(8,128)S(1)}, bf16[768,512]{1,0:T(8,128)(2,1)S(1)}) custom-call(s32[32]{0:T(128)S(1)} %bitcast.25, bf16[2,16,32,768]{3,2,1,0:T(8,128)(2,1)S(1)} %bitcast.16, bf16[768,1024]{1,0:T(8,128)(2,1)S(1)} %bitcast.18, bf16[8,192,256]{2,1,0:T(8,128)(2,1)S(1)} %all_gather.3.mine_ref, bf16[8,192,256]{2,1,0:T(8,128)(2,1)S(1)} %collective-permute-done.other_ref), custom_call_target="tpu_custom_call" | custom-call | tf_op jit(solution)/shard_map/own/pallas_call | solution.py:300
  46.2 4.9 %collective-permute-done.1 = bf16[1024,768]{1,0:T(8,128)(2,1)S(1)} collective-permute-done((bf16[1024,768]{1,0:T(8,128)(2,1)}, bf16[1024,768]{1,0:T(8,128)(2,1)S(1)}, u32[]{:S(2)}, u32[]{:S(2)}) %collective-permute-start.1) | collective-permute-done | bytes 1572896 | tf_op jit(solution)/shard_map/ppermute | solution.py:294
  51.1 2.3 %pair.1 = bf16[16,64,512]{2,1,0:T(8,128)(2,1)} custom-call(s32[32]{0:T(128)S(1)} %bitcast.26, f32[1024,512]{1,0:T(8,128)S(1)} %get-tuple-element.10.part_ref, bf16[768,512]{1,0:T(8,128)(2,1)S(1)} %get-tuple-element.11.far_ref, bf16[2,16,32,768]{3,2,1,0:T(8,128)(2,1)S(1)} %bitcast.22), custom_call_target="tpu_custom_call" | custom-call | tf_op jit(solution)/shard_map/pair/pallas_call | solution.py:304
  53.4 11.9 %all-to-all-start.1 = ((bf16[16,64,512]{2,1,0:T(8,128)(2,1)}), bf16[16,64,512]{2,1,0:T(8,128)(2,1)S(1)}, u32[]{:S(2)}, u32[]{:S(2)}) async-start(bf16[16,64,512]{2,1,0:T(8,128)(2,1)} %pair.1), calls=%async_computation.1 | async-start | bytes 2097152 | tf_op jit(solution)/shard_map/all_to_all | solution.py:307
  65.4 0.1 add.75
  65.5 0.1 add.77
  65.5 0.1 and_select_fusion.bias_ref
  65.6 1.2 %copy-done.3 = bf16[1,32,16,1024]{3,2,1,0:T(8,128)(2,1)S(1)} copy-done((bf16[1,32,16,1024]{3,2,1,0:T(8,128)(2,1)S(1)}, bf16[1,32,16,1024]{3,2,1,0:T(8,128)(2,1)}, u32[]{:S(2)}) %copy-start.3) | copy-done | bytes 1048600
  66.9 1.3 %cache_part.1.acc_ref = f32[3120,128]{1,0:T(8,128)S(1)} custom-call(bf16[64,6144]{1,0:T(8,128)(2,1)S(1)} %bitcast.20, bf16[512,1024]{1,0:T(8,128)(2,1)S(1)} %bitcast.23, f32[32,256]{1,0:T(8,128)S(1)} %and_select_fusion.bias_ref), custom_call_target="tpu_custom_call" | custom-call | flops 402653184 | bytes 6291456 | tf_op jit(solution)/shard_map/cache_part/pallas_call | solution.py:104
  68.1 0.2 fusion
  68.3 0.1 pad_maximum_fusion
  68.4 0.1 and_select_fusion.1.bias_ref
  68.5 26.0 %all-to-all-done.1 = bf16[16,64,512]{2,1,0:T(8,128)(2,1)S(1)} async-done(((bf16[16,64,512]{2,1,0:T(8,128)(2,1)}), bf16[16,64,512]{2,1,0:T(8,128)(2,1)S(1)}, u32[]{:S(2)}, u32[]{:S(2)}) %all-to-all-start.1) | async-done | bytes 1048608 | tf_op jit(solution)/shard_map/all_to_all | solution.py:307
  94.5 2.9 %finish.1 = bf16[64,6144]{1,0:T(8,128)(2,1)} custom-call(bf16[64,6144]{1,0:T(8,128)(2,1)S(1)} %bitcast.21, bf16[8,2,64,512]{3,2,1,0:T(8,128)(2,1)S(1)} %bitcast.19, f32[64,128]{1,0:T(8,128)S(1)} %get-tuple-element.16.cos_ref, f32[64,128]{1,0:T(8,128)S(1)} %get-tuple-element.17.sin_ref, f32[32,32]{1,0:T(8,128)S(1)} %and_select_fusion.1.bias_ref, ...), custom_call_target="tpu_custom_call" | custom-call | tf_op jit(solution)/shard_map/finish/pallas_call | solution.py:127
  (15 shorter events, 0.1 us)
Async XLA Ops:
  1.4 10.1 %all-to-all-start = ((bf16[8,24,256]{2,1,0:T(8,128)(2,1)}), bf16[8,24,256]{2,1,0:T(8,128)(2,1)S(1)}, u32[]{:S(2)}, u32[]{:S(2)}) async-start(bf16[8,24,256]{2,1,0:T(8,128)(2,1)} %pieces.1), calls=%async_computation | async-start | bytes 196608 | tf_op jit(solution)/shard_map/all_to_all | solution.py:291
  5.7 38.9 %copy-start = (bf16[2,1,512,768]{3,2,1,0:T(8,128)(2,1)S(1)}, bf16[2,1,512,768]{3,2,1,0:T(8,128)(2,1)}, u32[]{:S(2)}) copy-start(bf16[2,1,512,768]{3,2,1,0:T(8,128)(2,1)} %param.7) | copy-start | bytes 4718596
  5.8 38.9 %copy-start.1 = (bf16[1,768,1024]{2,1,0:T(8,128)(2,1)S(1)}, bf16[1,768,1024]{2,1,0:T(8,128)(2,1)}, u32[]{:S(2)}) copy-start(bf16[1,768,1024]{2,1,0:T(8,128)(2,1)} %param.12) | copy-start | bytes 4718596
  5.8 38.8 %copy-start.4 = (s32[32,1]{0,1:T(1,128)S(1)}, s32[32,1]{0,1:T(1,128)}, u32[]{:S(2)}) copy-start(s32[32,1]{0,1:T(1,128)} %param.11) | copy-start | bytes 388
  11.5 39.6 %collective-permute-start.1 = (bf16[1024,768]{1,0:T(8,128)(2,1)}, bf16[1024,768]{1,0:T(8,128)(2,1)S(1)}, u32[]{:S(2)}, u32[]{:S(2)}) collective-permute-start(bf16[1024,768]{1,0:T(8,128)(2,1)} %outgoing.1), channel_id=1, source_target_pairs={{0,1},{1,0},{2,3},{3,2},{4,5},{5,4},{6,7},{7,6},{8,9},{9,8},{10,11... | collective-permute-start | bytes 4718600 | tf_op jit(solution)/shard_map/ppermute | solution.py:294
  40.4 4.2 %collective-permute-start = (bf16[8,192,256]{2,1,0:T(8,128)(2,1)S(1)}, bf16[8,192,256]{2,1,0:T(8,128)(2,1)S(1)}, u32[]{:S(2)}, u32[]{:S(2)}) collective-permute-start(bf16[8,192,256]{2,1,0:T(8,128)(2,1)S(1)} %all_gather.3.mine_ref), channel_id=1, source_target_pairs={{0,16},{16,0},{32,48},{48,32},{64,80},{80,64},{96,112},{112,96},{1... | collective-permute-start | bytes 2359304 | tf_op jit(solution)/shard_map/ppermute | solution.py:296
  53.4 11.9 %copy-start.5 = (s32[32]{0:T(128)S(1)}, s32[32]{0:T(128)}, u32[]{:S(2)}) copy-start(s32[32]{0:T(128)} %param.10) | copy-start | bytes 388
  53.4 12.2 %copy-start.2 = (bf16[2,1,32,6144]{3,2,1,0:T(8,128)(2,1)S(1)}, bf16[2,1,32,6144]{3,2,1,0:T(8,128)(2,1)}, u32[]{:S(2)}) copy-start(bf16[2,1,32,6144]{3,2,1,0:T(8,128)(2,1)} %param.8) | copy-start | bytes 2359300
  53.4 41.1 %all-to-all-start.1 = ((bf16[16,64,512]{2,1,0:T(8,128)(2,1)}), bf16[16,64,512]{2,1,0:T(8,128)(2,1)S(1)}, u32[]{:S(2)}, u32[]{:S(2)}) async-start(bf16[16,64,512]{2,1,0:T(8,128)(2,1)} %pair.1), calls=%async_computation.1 | async-start | bytes 2097152 | tf_op jit(solution)/shard_map/all_to_all | solution.py:307
  65.6 1.2 %copy-start.3 = (bf16[1,32,16,1024]{3,2,1,0:T(8,128)(2,1)S(1)}, bf16[1,32,16,1024]{3,2,1,0:T(8,128)(2,1)}, u32[]{:S(2)}) copy-start(bf16[1,32,16,1024]{3,2,1,0:T(8,128)(2,1)} %param.9) | copy-start | bytes 3145732

commit v4 on v3

--- a/solution.py
+++ b/solution.py
@@ -69,24 +69,23 @@
         k = (k*cos_ref[...] + pltpu.roll(k, HEAD//2, 1)*sin_ref[...]).astype(jnp.bfloat16)
         v = v.astype(jnp.bfloat16)
         v = jnp.concatenate([v, jnp.ones_like(v)], 1)
+        q = jnp.concatenate([_queries(q_ref, steps, rows, half*BLOCK, g) for half in range(rows//BLOCK)], 0)
+        every = q.shape[0]
+        s = lax.dot_general(q, k, (((1,), (1,)), ((), ())), preferred_element_type=jnp.float32) * SCALE
+        s = (s.reshape(rows//BLOCK, QPK, steps*BLOCK, steps*rows) + bias_ref[...][:, None]).reshape(every, steps*rows)
+        spot = lambda n: jnp.concatenate([jnp.broadcast_to(stat[:, 2*(half*KVH+g)+n:2*(half*KVH+g)+n+1], (n_rows, HEAD)) for half in range(rows//BLOCK)], 0)
+        n_rows = every // (rows//BLOCK)
+        old, total = spot(0), spot(1)
+        peak = jnp.maximum(old, jnp.max(s, -1, keepdims=True))
+        p = jnp.exp(s - peak[:, :steps*rows]).astype(jnp.bfloat16)
+        both = jnp.dot(p, v, preferred_element_type=jnp.float32)
+        keep = jnp.exp(old - peak)
+        out = (acc_ref[g*tall:(g+1)*tall, :]*keep + both[:, :HEAD]) / (total*keep + both[:, HEAD:])
+        out = out.astype(held.dtype)
         for half in range(rows//BLOCK):
-            q = _queries(q_ref, steps, rows, half*BLOCK, g)
-            pick = lambda x: jnp.concatenate([x[t*rows+half*BLOCK:t*rows+(half+1)*BLOCK] for t in range(steps)], 0)
-            s = lax.dot_general(q, pick(k), (((1,), (1,)), ((), ())), preferred_element_type=jnp.float32) * SCALE
-            s = (s.reshape(QPK, steps*BLOCK, steps*BLOCK) + bias_ref[...][None]).reshape(n, steps*BLOCK)
-            at = slice(half*n, (half+1)*n)
-            spot = 2*(half*KVH+g)
-            old = jnp.broadcast_to(stat[:, spot:spot+1], (n, HEAD))
-            total = jnp.broadcast_to(stat[:, spot+1:spot+2], (n, HEAD))
-            peak = jnp.maximum(old, jnp.max(s, -1, keepdims=True))
-            p = jnp.exp(s - peak[:, :steps*BLOCK]).astype(jnp.bfloat16)
-            both = jnp.dot(p, pick(v), preferred_element_type=jnp.float32)
-            keep = jnp.exp(old - peak)
-            out = (acc_ref[g*tall+half*n:g*tall+(half+1)*n, :]*keep + both[:, :HEAD]) / (total*keep + both[:, HEAD:])
-            out = out.astype(held.dtype)
             for j in range(QPK):
                 for t in range(steps):
-                    b = (j*steps+t)*BLOCK
+                    b = half*n_rows+(j*steps+t)*BLOCK
                     held[t*rows+half*BLOCK:t*rows+(half+1)*BLOCK, g*WIDE+j*HEAD:g*WIDE+(j+1)*HEAD] = out[b:b+BLOCK]
         part = slice(g*WIDE, (g+1)*WIDE)
         copies.append(pltpu.make_async_copy(held.at[:, part], out_ref.at[:, part], sems.at[g]))
@@ -119,8 +118,8 @@
 
 def finish(q, kv_sum, cos, sin, stats):
     steps, rows, width = q.shape
-    at = jnp.arange(steps*BLOCK, dtype=jnp.int32)
-    ok = (at[:, None] % BLOCK == at[None] % BLOCK) & (at[None]//BLOCK <= at[:, None]//BLOCK)
+    half, at, key = (lax.broadcasted_iota(jnp.int32, (rows//BLOCK, steps*BLOCK, steps*rows), d) for d in range(3))
+    ok = (half*BLOCK + at % BLOCK == key % rows) & (key//rows <= at//BLOCK)
     bias = jnp.where(ok, 0.0, MASKED).astype(jnp.float32)
     n = steps*rows
     pieces = kv_sum.shape[0]//2
@@ -203,7 +202,7 @@
     )(served, x, resident)
 
 
-def own_kernel(versions_ref, own_ref, resident_ref, mine_ref, other_ref, part_ref, far_ref, near):
+def own_kernel(versions_ref, own_ref, resident_ref, mine_ref, other_ref, part_ref, far_ref, fresh_ref, near):
     depth, wide = far_ref.shape
     steps, shards = own_ref.shape[:2]
     ycount, tall, quarter = mine_ref.shape
@@ -211,6 +210,7 @@
     high, core = lax.axis_index("tensor") % 2, lax.axis_index("replica") % 2
     fresh = versions_ref[lax.axis_index("replica")] == 1
     blocks = CHUNK // (steps * own_ref.shape[2])
+    fresh_ref[...] = jnp.full(fresh_ref.shape, versions_ref[lax.axis_index("replica")], jnp.int32)
 
     def run(weight):
         for i in range(0, shards, blocks):
@@ -234,10 +234,10 @@
         run(resident_ref[:, pl.ds(pl.multiple_of(high * wide, wide), wide)])
 
 
-def pair_kernel(versions_ref, part_ref, far_ref, pair_ref, out_ref, held, sems):
+def pair_kernel(fresh_ref, part_ref, far_ref, pair_ref, out_ref, held, sems):
     wide = far_ref.shape[1]
     steps, shards = pair_ref.shape[:2]
-    fresh = versions_ref[lax.axis_index("replica")] == 1
+    fresh = jnp.max(fresh_ref[...]) == 1
     blocks = CHUNK // (steps * pair_ref.shape[2])
 
     def rows(i, cols):
@@ -297,12 +297,13 @@
     local = rows // shards
     shape = (shards, steps * local, wide)
     part = [jax.ShapeDtypeStruct((steps * rows, wide), jnp.float32), jax.ShapeDtypeStruct((width, wide), kind)]
-    part, far = call(own_kernel, [SM] + [VM] * 4, [VM] * 2, part, [pltpu.VMEM((width, wide), kind)], "own")(
+    part.append(jax.ShapeDtypeStruct((8, 128), jnp.int32))
+    part, far, fresh = call(own_kernel, [SM] + [VM] * 4, [VM] * 3, part, [pltpu.VMEM((width, wide), kind)], "own")(
         served, hidden.reshape(steps, shards, local, width), resident[0], mine, other
     )
     scratch = [pltpu.VMEM(shape, kind), pltpu.SemaphoreType.DMA((steps * rows // CHUNK,))]
-    partial = call(pair_kernel, [SM] + [VM] * 3, ANY, pltpu.HBM(shape, kind), scratch, "pair")(
-        served, part, far, pair.reshape(steps, shards, local, width)
+    partial = call(pair_kernel, [VM] * 4, ANY, pltpu.HBM(shape, kind), scratch, "pair")(
+        fresh, part, far, pair.reshape(steps, shards, local, width)
     )
     summands = lax.all_to_all(partial, "tensor", 0, 0, tiled=True)
     stats = cache_part(queries[:, 0], kv_cache[0], lengths)

time: 97.8 us -> 97.2 us (level)
  no operation moved by 1% of the time
where the time goes in v4:
time: 97.2 us; the launch traced here: 96.8 us
  waiting for transfers between devices  36 us (37%)
  blocking collectives  26.3 us (27%)
  starting transfers between devices  20.9 us (22%)
  Pallas kernels  11.5 us (12%)
  local copies, waits for them, and re-layouts  1.42 us (1%)
    all_gather x1, blocking collectives, per_device(): lax.all_gather(got.reshape(-1, wide // 2), 'replica', axis=0, axis_index_...  26.3 us
    all_to_all x1, waiting for transfers between devices, per_device(): summands = lax.all_to_all(partial, 'tensor', 0, 0, tiled=True)  25.9 us
    all_to_all x1, starting transfers between devices, per_device(): summands = lax.all_to_all(partial, 'tensor', 0, 0, tiled=True)  11.9 us
    ppermute x1, waiting for transfers between devices, per_device(): pair = lax.ppermute(message, 'tensor', [(i, i ^ 1) for i in range(shards)])  4.65 us
    all_to_all x1, starting transfers between devices, per_device(): lax.all_to_all(pieces, both, 0, 0, axis_index_groups=groups, tiled=True)  4.3 us
    all_to_all x1, waiting for transfers between devices, per_device(): lax.all_to_all(pieces, both, 0, 0, axis_index_groups=groups, tiled=True)  3.14 us
    ppermute x1, starting transfers between devices, per_device(): pair = lax.ppermute(message, 'tensor', [(i, i ^ 1) for i in range(shards)])  2.8 us
    pallas_call x1, Pallas kernels, finish(): pl.pallas_call(functools.partial(finish_kernel, steps=steps, rows=rows),...  2.65 us
  transfers between devices with their start and end apart: 4, of which 4 were waited for; matrix products, arithmetic and copies ran while one was open for 1% of the time, Pallas kernels for 6%

profile of v4, /device:TPU:32, one launch (start us, length us, event | category | flops | bytes accessed | tf_op | source)
XLA Modules:
  0.0 96.8 jit_solution(9358361186462555308)
XLA Ops:
  0.0 1.4 %pieces.1 = bf16[8,24,256]{2,1,0:T(8,128)(2,1)} custom-call(bf16[24,1024]{1,0:T(8,128)(2,1)} %bitcast.27), custom_call_target="tpu_custom_call" | custom-call | tf_op jit(solution)/shard_map/pieces/pallas_call | solution.py:290
  1.4 4.3 %all-to-all-start = ((bf16[8,24,256]{2,1,0:T(8,128)(2,1)}), bf16[8,24,256]{2,1,0:T(8,128)(2,1)S(1)}, u32[]{:S(2)}, u32[]{:S(2)}) async-start(bf16[8,24,256]{2,1,0:T(8,128)(2,1)} %pieces.1), calls=%async_computation | async-start | bytes 196608 | tf_op jit(solution)/shard_map/all_to_all | solution.py:291
  5.8 0.0 copy-start.4
  5.8 2.6 %outgoing.1 = bf16[1024,768]{1,0:T(8,128)(2,1)} custom-call(s32[32]{0:T(128)} %bitcast.24, bf16[1024,768]{1,0:T(8,128)(2,1)} %bitcast.15, bf16[768,1024]{1,0:T(8,128)(2,1)} %bitcast.17), custom_call_target="tpu_custom_call" | custom-call | tf_op jit(solution)/shard_map/outgoing/pallas_call | solution.py:189
  8.4 3.1 %all-to-all-done = bf16[8,24,256]{2,1,0:T(8,128)(2,1)S(1)} async-done(((bf16[8,24,256]{2,1,0:T(8,128)(2,1)}), bf16[8,24,256]{2,1,0:T(8,128)(2,1)S(1)}, u32[]{:S(2)}, u32[]{:S(2)}) %all-to-all-start) | async-done | bytes 98336 | tf_op jit(solution)/shard_map/all_to_all | solution.py:291
  11.5 2.8 %collective-permute-start.1 = (bf16[1024,768]{1,0:T(8,128)(2,1)}, bf16[1024,768]{1,0:T(8,128)(2,1)S(1)}, u32[]{:S(2)}, u32[]{:S(2)}) collective-permute-start(bf16[1024,768]{1,0:T(8,128)(2,1)} %outgoing.1), channel_id=1, source_target_pairs={{0,1},{1,0},{2,3},{3,2},{4,5},{5,4},{6,7},{7,6},{8,9},{9,8},{10,11... | collective-permute-start | bytes 4718600 | tf_op jit(solution)/shard_map/ppermute | solution.py:294
  14.4 26.3 %all_gather.3.mine_ref = bf16[8,192,256]{2,1,0:T(8,128)(2,1)S(1)} all-gather(bf16[1,192,256]{2,1,0:T(8,128)(2,1)S(1)} %bitcast.26), channel_id=1, replica_groups={{0,32,64,96,128,160,192,224},{16,48,80,112,144,176,208,240},{256,288,32..., dimensions={0}, use_global_device_ids=true | all-gather | bytes 884736 | tf_op jit(solution)/shard_map/all_gather | solution.py:295
  40.6 1.9 %collective-permute-start = (bf16[8,192,256]{2,1,0:T(8,128)(2,1)S(1)}, bf16[8,192,256]{2,1,0:T(8,128)(2,1)S(1)}, u32[]{:S(2)}, u32[]{:S(2)}) collective-permute-start(bf16[8,192,256]{2,1,0:T(8,128)(2,1)S(1)} %all_gather.3.mine_ref), channel_id=1, source_target_pairs={{0,16},{16,0},{32,48},{48,32},{64,80},{80,64},{96,112},{112,96},{1... | collective-permute-start | bytes 2359304 | tf_op jit(solution)/shard_map/ppermute | solution.py:296
  42.6 2.2 %collective-permute-done.other_ref = bf16[8,192,256]{2,1,0:T(8,128)(2,1)S(1)} collective-permute-done((bf16[8,192,256]{2,1,0:T(8,128)(2,1)S(1)}, bf16[8,192,256]{2,1,0:T(8,128)(2,1)S(1)}, u32[]{:S(2)}, u32[]{:S(2)}) %collective-permute-start) | collective-permute-done | bytes 786464 | tf_op jit(solution)/shard_map/ppermute | solution.py:296
  44.8 1.6 %own.1 = (f32[1024,512]{1,0:T(8,128)S(1)}, bf16[768,512]{1,0:T(8,128)(2,1)S(1)}, s32[8,128]{1,0:T(8,128)S(1)}) custom-call(s32[32]{0:T(128)S(1)} %bitcast.25, bf16[2,16,32,768]{3,2,1,0:T(8,128)(2,1)S(1)} %bitcast.16, bf16[768,1024]{1,0:T(8,128)(2,1)S(1)} %bitcast.18, bf16[8,192,256]{2,1,0:T(8,128)(2,1)S(1)} %all_gather.3.mine_ref, ...), custom_call_target="tpu_custom_call" | custom-call | tf_op jit(solution)/shard_map/own/pallas_call | solution.py:301
  46.5 4.7 %collective-permute-done.1 = bf16[1024,768]{1,0:T(8,128)(2,1)S(1)} collective-permute-done((bf16[1024,768]{1,0:T(8,128)(2,1)}, bf16[1024,768]{1,0:T(8,128)(2,1)S(1)}, u32[]{:S(2)}, u32[]{:S(2)}) %collective-permute-start.1) | collective-permute-done | bytes 1572896 | tf_op jit(solution)/shard_map/ppermute | solution.py:294
  51.1 1.9 %pair.1 = bf16[16,64,512]{2,1,0:T(8,128)(2,1)} custom-call(s32[8,128]{1,0:T(8,128)S(1)} %get-tuple-element.11.fresh_ref, f32[1024,512]{1,0:T(8,128)S(1)} %get-tuple-element.12.part_ref, bf16[768,512]{1,0:T(8,128)(2,1)S(1)} %get-tuple-element.13.far_ref, bf16[2,16,32,768]{3,2,1,0:T(8,128)(2,1)S(1)} %bitcast.22), custom_call_target="tpu_custom_call" | custom-call | tf_op jit(solution)/shard_map/pair/pallas_call | solution.py:305
  53.0 0.0 copy-start.5
  53.1 11.9 %all-to-all-start.1 = ((bf16[16,64,512]{2,1,0:T(8,128)(2,1)}), bf16[16,64,512]{2,1,0:T(8,128)(2,1)S(1)}, u32[]{:S(2)}, u32[]{:S(2)}) async-start(bf16[16,64,512]{2,1,0:T(8,128)(2,1)} %pair.1), calls=%async_computation.1 | async-start | bytes 2097152 | tf_op jit(solution)/shard_map/all_to_all | solution.py:308
  65.0 0.1 add.69
  65.1 0.1 add.71
  65.2 0.1 and_select_fusion.bias_ref
  65.3 1.2 %copy-done.3 = bf16[1,32,16,1024]{3,2,1,0:T(8,128)(2,1)S(1)} copy-done((bf16[1,32,16,1024]{3,2,1,0:T(8,128)(2,1)S(1)}, bf16[1,32,16,1024]{3,2,1,0:T(8,128)(2,1)}, u32[]{:S(2)}) %copy-start.3) | copy-done | bytes 1048600
  66.5 1.2 %cache_part.1.acc_ref = f32[3120,128]{1,0:T(8,128)S(1)} custom-call(bf16[64,6144]{1,0:T(8,128)(2,1)S(1)} %bitcast.20, bf16[512,1024]{1,0:T(8,128)(2,1)S(1)} %bitcast.23, f32[32,256]{1,0:T(8,128)S(1)} %and_select_fusion.bias_ref), custom_call_target="tpu_custom_call" | custom-call | flops 402653184 | bytes 6291456 | tf_op jit(solution)/shard_map/cache_part/pallas_call | solution.py:103
  67.8 0.2 fusion.2
  68.0 0.1 pad_maximum_fusion
  68.1 0.1 fusion.1.bias_ref
  68.2 25.9 %all-to-all-done.1 = bf16[16,64,512]{2,1,0:T(8,128)(2,1)S(1)} async-done(((bf16[16,64,512]{2,1,0:T(8,128)(2,1)}), bf16[16,64,512]{2,1,0:T(8,128)(2,1)S(1)}, u32[]{:S(2)}, u32[]{:S(2)}) %all-to-all-start.1) | async-done | bytes 1048608 | tf_op jit(solution)/shard_map/all_to_all | solution.py:308
  94.2 2.6 %finish.1 = bf16[64,6144]{1,0:T(8,128)(2,1)} custom-call(bf16[64,6144]{1,0:T(8,128)(2,1)S(1)} %bitcast.21, bf16[8,2,64,512]{3,2,1,0:T(8,128)(2,1)S(1)} %bitcast.19, f32[64,128]{1,0:T(8,128)S(1)} %get-tuple-element.18.cos_ref, f32[64,128]{1,0:T(8,128)S(1)} %get-tuple-element.19.sin_ref, f32[2,32,64]{2,1,0:T(8,128)S(1)} %fusion.1.bias_ref, ...), custom_call_target="tpu_custom_call" | custom-call | tf_op jit(solution)/shard_map/finish/pallas_call | solution.py:126
  (22 shorter events, 0.1 us)
Async XLA Ops:
  1.4 10.1 %all-to-all-start = ((bf16[8,24,256]{2,1,0:T(8,128)(2,1)}), bf16[8,24,256]{2,1,0:T(8,128)(2,1)S(1)}, u32[]{:S(2)}, u32[]{:S(2)}) async-start(bf16[8,24,256]{2,1,0:T(8,128)(2,1)} %pieces.1), calls=%async_computation | async-start | bytes 196608 | tf_op jit(solution)/shard_map/all_to_all | solution.py:291
  5.7 39.1 %copy-start = (bf16[2,1,512,768]{3,2,1,0:T(8,128)(2,1)S(1)}, bf16[2,1,512,768]{3,2,1,0:T(8,128)(2,1)}, u32[]{:S(2)}) copy-start(bf16[2,1,512,768]{3,2,1,0:T(8,128)(2,1)} %param.7) | copy-start | bytes 4718596
  5.8 39.1 %copy-start.1 = (bf16[1,768,1024]{2,1,0:T(8,128)(2,1)S(1)}, bf16[1,768,1024]{2,1,0:T(8,128)(2,1)}, u32[]{:S(2)}) copy-start(bf16[1,768,1024]{2,1,0:T(8,128)(2,1)} %param.12) | copy-start | bytes 4718596
  5.8 39.1 %copy-start.4 = (s32[32,1]{0,1:T(1,128)S(1)}, s32[32,1]{0,1:T(1,128)}, u32[]{:S(2)}) copy-start(s32[32,1]{0,1:T(1,128)} %param.11) | copy-start | bytes 388
  11.5 39.6 %collective-permute-start.1 = (bf16[1024,768]{1,0:T(8,128)(2,1)}, bf16[1024,768]{1,0:T(8,128)(2,1)S(1)}, u32[]{:S(2)}, u32[]{:S(2)}) collective-permute-start(bf16[1024,768]{1,0:T(8,128)(2,1)} %outgoing.1), channel_id=1, source_target_pairs={{0,1},{1,0},{2,3},{3,2},{4,5},{5,4},{6,7},{7,6},{8,9},{9,8},{10,11... | collective-permute-start | bytes 4718600 | tf_op jit(solution)/shard_map/ppermute | solution.py:294
  40.6 4.2 %collective-permute-start = (bf16[8,192,256]{2,1,0:T(8,128)(2,1)S(1)}, bf16[8,192,256]{2,1,0:T(8,128)(2,1)S(1)}, u32[]{:S(2)}, u32[]{:S(2)}) collective-permute-start(bf16[8,192,256]{2,1,0:T(8,128)(2,1)S(1)} %all_gather.3.mine_ref), channel_id=1, source_target_pairs={{0,16},{16,0},{32,48},{48,32},{64,80},{80,64},{96,112},{112,96},{1... | collective-permute-start | bytes 2359304 | tf_op jit(solution)/shard_map/ppermute | solution.py:296
  53.0 11.9 %copy-start.5 = (s32[32]{0:T(128)S(1)}, s32[32]{0:T(128)}, u32[]{:S(2)}) copy-start(s32[32]{0:T(128)} %param.10) | copy-start | bytes 388
  53.1 12.2 %copy-start.2 = (bf16[2,1,32,6144]{3,2,1,0:T(8,128)(2,1)S(1)}, bf16[2,1,32,6144]{3,2,1,0:T(8,128)(2,1)}, u32[]{:S(2)}) copy-start(bf16[2,1,32,6144]{3,2,1,0:T(8,128)(2,1)} %param.8) | copy-start | bytes 2359300
  53.1 41.1 %all-to-all-start.1 = ((bf16[16,64,512]{2,1,0:T(8,128)(2,1)}), bf16[16,64,512]{2,1,0:T(8,128)(2,1)S(1)}, u32[]{:S(2)}, u32[]{:S(2)}) async-start(bf16[16,64,512]{2,1,0:T(8,128)(2,1)} %pair.1), calls=%async_computation.1 | async-start | bytes 2097152 | tf_op jit(solution)/shard_map/all_to_all | solution.py:308
  65.3 1.2 %copy-start.3 = (bf16[1,32,16,1024]{3,2,1,0:T(8,128)(2,1)S(1)}, bf16[1,32,16,1024]{3,2,1,0:T(8,128)(2,1)}, u32[]{:S(2)}) copy-start(bf16[1,32,16,1024]{3,2,1,0:T(8,128)(2,1)} %param.9) | copy-start | bytes 3145732

commit v5 on v4

--- a/solution.py
+++ b/solution.py
@@ -143,7 +143,7 @@
         out_ref[i] = update_ref[:, at * wide : (at + 1) * wide]
 
 
-def outgoing_kernel(served_ref, x_ref, resident_ref, out_ref, x_held, weight, versions_ref, sems, *, first):
+def outgoing_kernel(versions_ref, x_ref, resident_ref, out_ref, x_held, weight, sems, *, first):
     rows, depth = out_ref.shape
     wide = weight.shape[1]
     chunks = [slice(i, i + CHUNK) for i in range(0, rows, CHUNK)]
@@ -154,21 +154,20 @@
     leaving = [pltpu.make_async_copy(x_held.at[c], out_ref.at[c], sems.at[count + n]) for n, c in enumerate(chunks)]
     short = [pltpu.make_async_copy(x_held.at[c, :wide], out_ref.at[c, :wide], sems.at[count + n]) for n, c in enumerate(chunks)]
 
-    which = pltpu.make_async_copy(served_ref, versions_ref, sems.at[2 * count + 1])
-    which.start()
-    arrivals[0].start()
-    load.start()
-    for copy in arrivals[1:]:
+    fresh = versions_ref[lax.axis_index("replica")] == 1
+
+    @pl.when(jnp.logical_not(fresh))
+    def _():
+        load.start()
+
+    for copy in arrivals:
         copy.start()
-    which.wait()
-    fresh = versions_ref[lax.axis_index("replica")] == 1
 
     @pl.when(fresh)
     def _():
         for n in range(count):
             arrivals[n].wait()
             leaving[n].start()
-        load.wait()
         for copy in leaving:
             copy.wait()
 
@@ -188,14 +187,13 @@
     depth, wide = x.shape[1], resident.shape[1] // 2
     return pl.pallas_call(
         functools.partial(outgoing_kernel, first=first),
-        in_specs=[ANY] * 3,
+        in_specs=[SM] + [ANY] * 2,
         out_specs=ANY,
         out_shape=jax.ShapeDtypeStruct((rows, depth), x.dtype),
         scratch_shapes=[
             pltpu.VMEM((rows, depth), x.dtype),
             pltpu.VMEM((depth, wide), x.dtype),
-            pltpu.SMEM(served.shape, jnp.int32),
-            pltpu.SemaphoreType.DMA((2 * (rows // CHUNK) + 2,)),
+            pltpu.SemaphoreType.DMA((2 * (rows // CHUNK) + 1,)),
         ],
         compiler_params=pltpu.CompilerParams(vmem_limit_bytes=60 << 20),
         name="outgoing",

time: 97.2 us -> 97.6 us (level)
  the two profiles are of different devices: /device:TPU:32 before, /device:TPU:8 now
where the time goes in v5:
time: 97.6 us; the launch traced here: 97.2 us
  waiting for transfers between devices  33.3 us (34%)
  blocking collectives  28.7 us (29%)
  starting transfers between devices  20.9 us (21%)
  Pallas kernels  12 us (12%)
  local copies, waits for them, and re-layouts  1.42 us (1%)
    all_gather x1, blocking collectives, per_device(): lax.all_gather(got.reshape(-1, wide // 2), 'replica', axis=0, axis_index_...  28.7 us
    all_to_all x1, waiting for transfers between devices, per_device(): summands = lax.all_to_all(partial, 'tensor', 0, 0, tiled=True)  26.3 us
    all_to_all x1, starting transfers between devices, per_device(): summands = lax.all_to_all(partial, 'tensor', 0, 0, tiled=True)  11.9 us
    all_to_all x1, starting transfers between devices, per_device(): lax.all_to_all(pieces, both, 0, 0, axis_index_groups=groups, tiled=True)  4.3 us
    pallas_call x1, Pallas kernels, outgoing(): pl.pallas_call(functools.partial(outgoing_kernel, first=first), in_specs=...  3.17 us
    ppermute x1, starting transfers between devices, per_device(): pair = lax.ppermute(message, 'tensor', [(i, i ^ 1) for i in range(shards)])  2.86 us
    pallas_call x1, Pallas kernels, finish(): pl.pallas_call(functools.partial(finish_kernel, steps=steps, rows=rows),...  2.65 us
    all_to_all x1, waiting for transfers between devices, per_device(): lax.all_to_all(pieces, both, 0, 0, axis_index_groups=groups, tiled=True)  2.59 us
  transfers between devices with their start and end apart: 4, of which 4 were waited for; matrix products, arithmetic and copies ran while one was open for 1% of the time, Pallas kernels for 6%

profile of v5, /device:TPU:8, one launch (start us, length us, event | category | flops | bytes accessed | tf_op | source)
XLA Modules:
  0.0 97.2 jit_solution(4094148807384079826)
XLA Ops:
  0.0 1.4 %pieces.1 = bf16[8,24,256]{2,1,0:T(8,128)(2,1)} custom-call(bf16[24,1024]{1,0:T(8,128)(2,1)} %bitcast.27), custom_call_target="tpu_custom_call" | custom-call | tf_op jit(solution)/shard_map/pieces/pallas_call | solution.py:288
  1.4 4.3 %all-to-all-start = ((bf16[8,24,256]{2,1,0:T(8,128)(2,1)}), bf16[8,24,256]{2,1,0:T(8,128)(2,1)S(1)}, u32[]{:S(2)}, u32[]{:S(2)}) async-start(bf16[8,24,256]{2,1,0:T(8,128)(2,1)} %pieces.1), calls=%async_computation | async-start | bytes 196608 | tf_op jit(solution)/shard_map/all_to_all | solution.py:289
  5.8 0.0 copy-start.1
  5.8 3.2 %outgoing.1 = bf16[1024,768]{1,0:T(8,128)(2,1)} custom-call(s32[32]{0:T(128)} %bitcast.24, bf16[1024,768]{1,0:T(8,128)(2,1)} %bitcast.15, bf16[768,1024]{1,0:T(8,128)(2,1)} %bitcast.17), custom_call_target="tpu_custom_call" | custom-call | tf_op jit(solution)/shard_map/outgoing/pallas_call | solution.py:188
  9.0 2.6 %all-to-all-done = bf16[8,24,256]{2,1,0:T(8,128)(2,1)S(1)} async-done(((bf16[8,24,256]{2,1,0:T(8,128)(2,1)}), bf16[8,24,256]{2,1,0:T(8,128)(2,1)S(1)}, u32[]{:S(2)}, u32[]{:S(2)}) %all-to-all-start) | async-done | bytes 98336 | tf_op jit(solution)/shard_map/all_to_all | solution.py:289
  11.5 2.9 %collective-permute-start.1 = (bf16[1024,768]{1,0:T(8,128)(2,1)}, bf16[1024,768]{1,0:T(8,128)(2,1)S(1)}, u32[]{:S(2)}, u32[]{:S(2)}) collective-permute-start(bf16[1024,768]{1,0:T(8,128)(2,1)} %outgoing.1), channel_id=1, source_target_pairs={{0,1},{1,0},{2,3},{3,2},{4,5},{5,4},{6,7},{7,6},{8,9},{9,8},{10,11... | collective-permute-start | bytes 4718600 | tf_op jit(solution)/shard_map/ppermute | solution.py:292
  14.4 28.7 %all_gather.3.mine_ref = bf16[8,192,256]{2,1,0:T(8,128)(2,1)S(1)} all-gather(bf16[1,192,256]{2,1,0:T(8,128)(2,1)S(1)} %bitcast.26), channel_id=1, replica_groups={{0,32,64,96,128,160,192,224},{16,48,80,112,144,176,208,240},{256,288,32..., dimensions={0}, use_global_device_ids=true | all-gather | bytes 884736 | tf_op jit(solution)/shard_map/all_gather | solution.py:293
  43.1 1.9 %collective-permute-start = (bf16[8,192,256]{2,1,0:T(8,128)(2,1)S(1)}, bf16[8,192,256]{2,1,0:T(8,128)(2,1)S(1)}, u32[]{:S(2)}, u32[]{:S(2)}) collective-permute-start(bf16[8,192,256]{2,1,0:T(8,128)(2,1)S(1)} %all_gather.3.mine_ref), channel_id=1, source_target_pairs={{0,16},{16,0},{32,48},{48,32},{64,80},{80,64},{96,112},{112,96},{1... | collective-permute-start | bytes 2359304 | tf_op jit(solution)/shard_map/ppermute | solution.py:294
  45.1 2.2 %collective-permute-done.other_ref = bf16[8,192,256]{2,1,0:T(8,128)(2,1)S(1)} collective-permute-done((bf16[8,192,256]{2,1,0:T(8,128)(2,1)S(1)}, bf16[8,192,256]{2,1,0:T(8,128)(2,1)S(1)}, u32[]{:S(2)}, u32[]{:S(2)}) %collective-permute-start) | collective-permute-done | bytes 786464 | tf_op jit(solution)/shard_map/ppermute | solution.py:294
  47.3 1.6 %own.1 = (f32[1024,512]{1,0:T(8,128)S(1)}, bf16[768,512]{1,0:T(8,128)(2,1)S(1)}, s32[8,128]{1,0:T(8,128)S(1)}) custom-call(s32[32]{0:T(128)S(1)} %bitcast.25, bf16[2,16,32,768]{3,2,1,0:T(8,128)(2,1)S(1)} %bitcast.16, bf16[768,1024]{1,0:T(8,128)(2,1)S(1)} %bitcast.18, bf16[8,192,256]{2,1,0:T(8,128)(2,1)S(1)} %all_gather.3.mine_ref, ...), custom_call_target="tpu_custom_call" | custom-call | tf_op jit(solution)/shard_map/own/pallas_call | solution.py:299
  49.0 2.2 %collective-permute-done.1 = bf16[1024,768]{1,0:T(8,128)(2,1)S(1)} collective-permute-done((bf16[1024,768]{1,0:T(8,128)(2,1)}, bf16[1024,768]{1,0:T(8,128)(2,1)S(1)}, u32[]{:S(2)}, u32[]{:S(2)}) %collective-permute-start.1) | collective-permute-done | bytes 1572896 | tf_op jit(solution)/shard_map/ppermute | solution.py:292
  51.1 1.9 %pair.1 = bf16[16,64,512]{2,1,0:T(8,128)(2,1)} custom-call(s32[8,128]{1,0:T(8,128)S(1)} %get-tuple-element.11.fresh_ref, f32[1024,512]{1,0:T(8,128)S(1)} %get-tuple-element.12.part_ref, bf16[768,512]{1,0:T(8,128)(2,1)S(1)} %get-tuple-element.13.far_ref, bf16[2,16,32,768]{3,2,1,0:T(8,128)(2,1)S(1)} %bitcast.22), custom_call_target="tpu_custom_call" | custom-call | tf_op jit(solution)/shard_map/pair/pallas_call | solution.py:303
  53.0 0.0 copy-start.5
  53.1 11.9 %all-to-all-start.1 = ((bf16[16,64,512]{2,1,0:T(8,128)(2,1)}), bf16[16,64,512]{2,1,0:T(8,128)(2,1)S(1)}, u32[]{:S(2)}, u32[]{:S(2)}) async-start(bf16[16,64,512]{2,1,0:T(8,128)(2,1)} %pair.1), calls=%async_computation.1 | async-start | bytes 2097152 | tf_op jit(solution)/shard_map/all_to_all | solution.py:306
  65.0 0.1 add.69
  65.1 0.1 add.71
  65.2 0.1 and_select_fusion.bias_ref
  65.3 1.2 %copy-done.3 = bf16[1,32,16,1024]{3,2,1,0:T(8,128)(2,1)S(1)} copy-done((bf16[1,32,16,1024]{3,2,1,0:T(8,128)(2,1)S(1)}, bf16[1,32,16,1024]{3,2,1,0:T(8,128)(2,1)}, u32[]{:S(2)}) %copy-start.3) | copy-done | bytes 1048600
  66.5 1.2 %cache_part.1.acc_ref = f32[3120,128]{1,0:T(8,128)S(1)} custom-call(bf16[64,6144]{1,0:T(8,128)(2,1)S(1)} %bitcast.20, bf16[512,1024]{1,0:T(8,128)(2,1)S(1)} %bitcast.23, f32[32,256]{1,0:T(8,128)S(1)} %and_select_fusion.bias_ref), custom_call_target="tpu_custom_call" | custom-call | flops 402653184 | bytes 6291456 | tf_op jit(solution)/shard_map/cache_part/pallas_call | solution.py:103
  67.8 0.2 fusion.2
  68.0 0.1 pad_maximum_fusion
  68.1 0.1 fusion.1.bias_ref
  68.2 26.3 %all-to-all-done.1 = bf16[16,64,512]{2,1,0:T(8,128)(2,1)S(1)} async-done(((bf16[16,64,512]{2,1,0:T(8,128)(2,1)}), bf16[16,64,512]{2,1,0:T(8,128)(2,1)S(1)}, u32[]{:S(2)}, u32[]{:S(2)}) %all-to-all-start.1) | async-done | bytes 1048608 | tf_op jit(solution)/shard_map/all_to_all | solution.py:306
  94.5 2.6 %finish.1 = bf16[64,6144]{1,0:T(8,128)(2,1)} custom-call(bf16[64,6144]{1,0:T(8,128)(2,1)S(1)} %bitcast.21, bf16[8,2,64,512]{3,2,1,0:T(8,128)(2,1)S(1)} %bitcast.19, f32[64,128]{1,0:T(8,128)S(1)} %get-tuple-element.18.cos_ref, f32[64,128]{1,0:T(8,128)S(1)} %get-tuple-element.19.sin_ref, f32[2,32,64]{2,1,0:T(8,128)S(1)} %fusion.1.bias_ref, ...), custom_call_target="tpu_custom_call" | custom-call | tf_op jit(solution)/shard_map/finish/pallas_call | solution.py:126
  (22 shorter events, 0.1 us)
Async XLA Ops:
  1.4 10.1 %all-to-all-start = ((bf16[8,24,256]{2,1,0:T(8,128)(2,1)}), bf16[8,24,256]{2,1,0:T(8,128)(2,1)S(1)}, u32[]{:S(2)}, u32[]{:S(2)}) async-start(bf16[8,24,256]{2,1,0:T(8,128)(2,1)} %pieces.1), calls=%async_computation | async-start | bytes 196608 | tf_op jit(solution)/shard_map/all_to_all | solution.py:289
  5.7 41.6 %copy-start = (bf16[2,1,512,768]{3,2,1,0:T(8,128)(2,1)S(1)}, bf16[2,1,512,768]{3,2,1,0:T(8,128)(2,1)}, u32[]{:S(2)}) copy-start(bf16[2,1,512,768]{3,2,1,0:T(8,128)(2,1)} %param.7) | copy-start | bytes 4718596
  5.8 41.5 %copy-start.1 = (bf16[1,768,1024]{2,1,0:T(8,128)(2,1)S(1)}, bf16[1,768,1024]{2,1,0:T(8,128)(2,1)}, u32[]{:S(2)}) copy-start(bf16[1,768,1024]{2,1,0:T(8,128)(2,1)} %param.12) | copy-start | bytes 4718596
  5.8 41.5 %copy-start.4 = (s32[32,1]{0,1:T(1,128)S(1)}, s32[32,1]{0,1:T(1,128)}, u32[]{:S(2)}) copy-start(s32[32,1]{0,1:T(1,128)} %param.11) | copy-start | bytes 388
  11.5 39.6 %collective-permute-start.1 = (bf16[1024,768]{1,0:T(8,128)(2,1)}, bf16[1024,768]{1,0:T(8,128)(2,1)S(1)}, u32[]{:S(2)}, u32[]{:S(2)}) collective-permute-start(bf16[1024,768]{1,0:T(8,128)(2,1)} %outgoing.1), channel_id=1, source_target_pairs={{0,1},{1,0},{2,3},{3,2},{4,5},{5,4},{6,7},{7,6},{8,9},{9,8},{10,11... | collective-permute-start | bytes 4718600 | tf_op jit(solution)/shard_map/ppermute | solution.py:292
  43.1 4.2 %collective-permute-start = (bf16[8,192,256]{2,1,0:T(8,128)(2,1)S(1)}, bf16[8,192,256]{2,1,0:T(8,128)(2,1)S(1)}, u32[]{:S(2)}, u32[]{:S(2)}) collective-permute-start(bf16[8,192,256]{2,1,0:T(8,128)(2,1)S(1)} %all_gather.3.mine_ref), channel_id=1, source_target_pairs={{0,16},{16,0},{32,48},{48,32},{64,80},{80,64},{96,112},{112,96},{1... | collective-permute-start | bytes 2359304 | tf_op jit(solution)/shard_map/ppermute | solution.py:294
  53.0 11.9 %copy-start.5 = (s32[32]{0:T(128)S(1)}, s32[32]{0:T(128)}, u32[]{:S(2)}) copy-start(s32[32]{0:T(128)} %param.10) | copy-start | bytes 388
  53.1 12.2 %copy-start.2 = (bf16[2,1,32,6144]{3,2,1,0:T(8,128)(2,1)S(1)}, bf16[2,1,32,6144]{3,2,1,0:T(8,128)(2,1)}, u32[]{:S(2)}) copy-start(bf16[2,1,32,6144]{3,2,1,0:T(8,128)(2,1)} %param.8) | copy-start | bytes 2359300
  53.1 41.4 %all-to-all-start.1 = ((bf16[16,64,512]{2,1,0:T(8,128)(2,1)}), bf16[16,64,512]{2,1,0:T(8,128)(2,1)S(1)}, u32[]{:S(2)}, u32[]{:S(2)}) async-start(bf16[16,64,512]{2,1,0:T(8,128)(2,1)} %pair.1), calls=%async_computation.1 | async-start | bytes 2097152 | tf_op jit(solution)/shard_map/all_to_all | solution.py:306
  65.2 1.2 %copy-start.3 = (bf16[1,32,16,1024]{3,2,1,0:T(8,128)(2,1)S(1)}, bf16[1,32,16,1024]{3,2,1,0:T(8,128)(2,1)}, u32[]{:S(2)}) copy-start(bf16[1,32,16,1024]{3,2,1,0:T(8,128)(2,1)} %param.9) | copy-start | bytes 3145732

commit v6 on v4

--- a/solution.py
+++ b/solution.py
@@ -59,6 +59,7 @@
     tall = QPK*steps*rows
     spots = 2*KVH*(rows//BLOCK)
     stat = jnp.concatenate([acc_ref[KVH*tall+k*spots:KVH*tall+(k+1)*spots, :] for k in range(n//HEAD)], 1).T
+    staged = []
     for g in range(KVH):
         cols = slice(g*HEAD, (g+1)*HEAD)
         k = sum_ref[0, 0, :, cols].astype(jnp.float32)
@@ -73,6 +74,9 @@
         every = q.shape[0]
         s = lax.dot_general(q, k, (((1,), (1,)), ((), ())), preferred_element_type=jnp.float32) * SCALE
         s = (s.reshape(rows//BLOCK, QPK, steps*BLOCK, steps*rows) + bias_ref[...][:, None]).reshape(every, steps*rows)
+        staged.append((s, v, every))
+    for g in range(KVH):
+        s, v, every = staged[g]
         spot = lambda n: jnp.concatenate([jnp.broadcast_to(stat[:, 2*(half*KVH+g)+n:2*(half*KVH+g)+n+1], (n_rows, HEAD)) for half in range(rows//BLOCK)], 0)
         n_rows = every // (rows//BLOCK)
         old, total = spot(0), spot(1)

time: 97.2 us -> 97.1 us (level)
  the two profiles are of different devices: /device:TPU:32 before, /device:TPU:24 now
where the time goes in v6:
time: 97.1 us; the launch traced here: 96.7 us
  waiting for transfers between devices  35.5 us (37%)
  blocking collectives  26.8 us (28%)
  starting transfers between devices  20.9 us (22%)
  Pallas kernels  11.4 us (12%)
  local copies, waits for them, and re-layouts  1.42 us (1%)
    all_gather x1, blocking collectives, per_device(): lax.all_gather(got.reshape(-1, wide // 2), 'replica', axis=0, axis_index_...  26.8 us
    all_to_all x1, waiting for transfers between devices, per_device(): summands = lax.all_to_all(partial, 'tensor', 0, 0, tiled=True)  25.9 us
    all_to_all x1, starting transfers between devices, per_device(): summands = lax.all_to_all(partial, 'tensor', 0, 0, tiled=True)  11.9 us
    all_to_all x1, starting transfers between devices, per_device(): lax.all_to_all(pieces, both, 0, 0, axis_index_groups=groups, tiled=True)  4.3 us
    ppermute x1, waiting for transfers between devices, per_device(): pair = lax.ppermute(message, 'tensor', [(i, i ^ 1) for i in range(shards)])  4.13 us
    all_to_all x1, waiting for transfers between devices, per_device(): lax.all_to_all(pieces, both, 0, 0, axis_index_groups=groups, tiled=True)  3.14 us
    ppermute x1, starting transfers between devices, per_device(): pair = lax.ppermute(message, 'tensor', [(i, i ^ 1) for i in range(shards)])  2.8 us
    pallas_call x1, Pallas kernels, outgoing(): pl.pallas_call(functools.partial(outgoing_kernel, first=first), in_specs=...  2.62 us
  transfers between devices with their start and end apart: 4, of which 4 were waited for; matrix products, arithmetic and copies ran while one was open for 1% of the time, Pallas kernels for 6%

profile of v6, /device:TPU:24, one launch (start us, length us, event | category | flops | bytes accessed | tf_op | source)
XLA Modules:
  0.0 96.7 jit_solution(11984156814977867624)
XLA Ops:
  0.0 1.4 %pieces.1 = bf16[8,24,256]{2,1,0:T(8,128)(2,1)} custom-call(bf16[24,1024]{1,0:T(8,128)(2,1)} %bitcast.27), custom_call_target="tpu_custom_call" | custom-call | tf_op jit(solution)/shard_map/pieces/pallas_call | solution.py:294
  1.4 4.3 %all-to-all-start = ((bf16[8,24,256]{2,1,0:T(8,128)(2,1)}), bf16[8,24,256]{2,1,0:T(8,128)(2,1)S(1)}, u32[]{:S(2)}, u32[]{:S(2)}) async-start(bf16[8,24,256]{2,1,0:T(8,128)(2,1)} %pieces.1), calls=%async_computation | async-start | bytes 196608 | tf_op jit(solution)/shard_map/all_to_all | solution.py:295
  5.8 0.0 copy-start.1
  5.8 0.0 copy-start.4
  5.8 2.6 %outgoing.1 = bf16[1024,768]{1,0:T(8,128)(2,1)} custom-call(s32[32]{0:T(128)} %bitcast.24, bf16[1024,768]{1,0:T(8,128)(2,1)} %bitcast.15, bf16[768,1024]{1,0:T(8,128)(2,1)} %bitcast.17), custom_call_target="tpu_custom_call" | custom-call | tf_op jit(solution)/shard_map/outgoing/pallas_call | solution.py:193
  8.4 3.1 %all-to-all-done = bf16[8,24,256]{2,1,0:T(8,128)(2,1)S(1)} async-done(((bf16[8,24,256]{2,1,0:T(8,128)(2,1)}), bf16[8,24,256]{2,1,0:T(8,128)(2,1)S(1)}, u32[]{:S(2)}, u32[]{:S(2)}) %all-to-all-start) | async-done | bytes 98336 | tf_op jit(solution)/shard_map/all_to_all | solution.py:295
  11.5 2.8 %collective-permute-start.1 = (bf16[1024,768]{1,0:T(8,128)(2,1)}, bf16[1024,768]{1,0:T(8,128)(2,1)S(1)}, u32[]{:S(2)}, u32[]{:S(2)}) collective-permute-start(bf16[1024,768]{1,0:T(8,128)(2,1)} %outgoing.1), channel_id=1, source_target_pairs={{0,1},{1,0},{2,3},{3,2},{4,5},{5,4},{6,7},{7,6},{8,9},{9,8},{10,11... | collective-permute-start | bytes 4718600 | tf_op jit(solution)/shard_map/ppermute | solution.py:298
  14.4 26.8 %all_gather.3.mine_ref = bf16[8,192,256]{2,1,0:T(8,128)(2,1)S(1)} all-gather(bf16[1,192,256]{2,1,0:T(8,128)(2,1)S(1)} %bitcast.26), channel_id=1, replica_groups={{0,32,64,96,128,160,192,224},{16,48,80,112,144,176,208,240},{256,288,32..., dimensions={0}, use_global_device_ids=true | all-gather | bytes 884736 | tf_op jit(solution)/shard_map/all_gather | solution.py:299
  41.2 1.9 %collective-permute-start = (bf16[8,192,256]{2,1,0:T(8,128)(2,1)S(1)}, bf16[8,192,256]{2,1,0:T(8,128)(2,1)S(1)}, u32[]{:S(2)}, u32[]{:S(2)}) collective-permute-start(bf16[8,192,256]{2,1,0:T(8,128)(2,1)S(1)} %all_gather.3.mine_ref), channel_id=1, source_target_pairs={{0,16},{16,0},{32,48},{48,32},{64,80},{80,64},{96,112},{112,96},{1... | collective-permute-start | bytes 2359304 | tf_op jit(solution)/shard_map/ppermute | solution.py:300
  43.1 2.2 %collective-permute-done.other_ref = bf16[8,192,256]{2,1,0:T(8,128)(2,1)S(1)} collective-permute-done((bf16[8,192,256]{2,1,0:T(8,128)(2,1)S(1)}, bf16[8,192,256]{2,1,0:T(8,128)(2,1)S(1)}, u32[]{:S(2)}, u32[]{:S(2)}) %collective-permute-start) | collective-permute-done | bytes 786464 | tf_op jit(solution)/shard_map/ppermute | solution.py:300
  45.4 1.6 %own.1 = (f32[1024,512]{1,0:T(8,128)S(1)}, bf16[768,512]{1,0:T(8,128)(2,1)S(1)}, s32[8,128]{1,0:T(8,128)S(1)}) custom-call(s32[32]{0:T(128)S(1)} %bitcast.25, bf16[2,16,32,768]{3,2,1,0:T(8,128)(2,1)S(1)} %bitcast.16, bf16[768,1024]{1,0:T(8,128)(2,1)S(1)} %bitcast.18, bf16[8,192,256]{2,1,0:T(8,128)(2,1)S(1)} %all_gather.3.mine_ref, ...), custom_call_target="tpu_custom_call" | custom-call | tf_op jit(solution)/shard_map/own/pallas_call | solution.py:305
  47.0 4.1 %collective-permute-done.1 = bf16[1024,768]{1,0:T(8,128)(2,1)S(1)} collective-permute-done((bf16[1024,768]{1,0:T(8,128)(2,1)}, bf16[1024,768]{1,0:T(8,128)(2,1)S(1)}, u32[]{:S(2)}, u32[]{:S(2)}) %collective-permute-start.1) | collective-permute-done | bytes 1572896 | tf_op jit(solution)/shard_map/ppermute | solution.py:298
  51.1 1.9 %pair.1 = bf16[16,64,512]{2,1,0:T(8,128)(2,1)} custom-call(s32[8,128]{1,0:T(8,128)S(1)} %get-tuple-element.11.fresh_ref, f32[1024,512]{1,0:T(8,128)S(1)} %get-tuple-element.12.part_ref, bf16[768,512]{1,0:T(8,128)(2,1)S(1)} %get-tuple-element.13.far_ref, bf16[2,16,32,768]{3,2,1,0:T(8,128)(2,1)S(1)} %bitcast.22), custom_call_target="tpu_custom_call" | custom-call | tf_op jit(solution)/shard_map/pair/pallas_call | solution.py:309
  53.1 11.9 %all-to-all-start.1 = ((bf16[16,64,512]{2,1,0:T(8,128)(2,1)}), bf16[16,64,512]{2,1,0:T(8,128)(2,1)S(1)}, u32[]{:S(2)}, u32[]{:S(2)}) async-start(bf16[16,64,512]{2,1,0:T(8,128)(2,1)} %pair.1), calls=%async_computation.1 | async-start | bytes 2097152 | tf_op jit(solution)/shard_map/all_to_all | solution.py:312
  65.0 0.1 add.69
  65.1 0.1 add.71
  65.2 0.1 and_select_fusion.bias_ref
  65.3 1.2 %copy-done.3 = bf16[1,32,16,1024]{3,2,1,0:T(8,128)(2,1)S(1)} copy-done((bf16[1,32,16,1024]{3,2,1,0:T(8,128)(2,1)S(1)}, bf16[1,32,16,1024]{3,2,1,0:T(8,128)(2,1)}, u32[]{:S(2)}) %copy-start.3) | copy-done | bytes 1048600
  66.5 1.2 %cache_part.1.acc_ref = f32[3120,128]{1,0:T(8,128)S(1)} custom-call(bf16[64,6144]{1,0:T(8,128)(2,1)S(1)} %bitcast.20, bf16[512,1024]{1,0:T(8,128)(2,1)S(1)} %bitcast.23, f32[32,256]{1,0:T(8,128)S(1)} %and_select_fusion.bias_ref), custom_call_target="tpu_custom_call" | custom-call | flops 402653184 | bytes 6291456 | tf_op jit(solution)/shard_map/cache_part/pallas_call | solution.py:107
  67.8 0.2 fusion.2
  68.0 0.1 pad_maximum_fusion
  68.1 0.1 fusion.1.bias_ref
  68.2 25.9 %all-to-all-done.1 = bf16[16,64,512]{2,1,0:T(8,128)(2,1)S(1)} async-done(((bf16[16,64,512]{2,1,0:T(8,128)(2,1)}), bf16[16,64,512]{2,1,0:T(8,128)(2,1)S(1)}, u32[]{:S(2)}, u32[]{:S(2)}) %all-to-all-start.1) | async-done | bytes 1048608 | tf_op jit(solution)/shard_map/all_to_all | solution.py:312
  94.2 2.5 %finish.1 = bf16[64,6144]{1,0:T(8,128)(2,1)} custom-call(bf16[64,6144]{1,0:T(8,128)(2,1)S(1)} %bitcast.21, bf16[8,2,64,512]{3,2,1,0:T(8,128)(2,1)S(1)} %bitcast.19, f32[64,128]{1,0:T(8,128)S(1)} %get-tuple-element.18.cos_ref, f32[64,128]{1,0:T(8,128)S(1)} %get-tuple-element.19.sin_ref, f32[2,32,64]{2,1,0:T(8,128)S(1)} %fusion.1.bias_ref, ...), custom_call_target="tpu_custom_call" | custom-call | tf_op jit(solution)/shard_map/finish/pallas_call | solution.py:130
  (22 shorter events, 0.1 us)
Async XLA Ops:
  1.4 10.1 %all-to-all-start = ((bf16[8,24,256]{2,1,0:T(8,128)(2,1)}), bf16[8,24,256]{2,1,0:T(8,128)(2,1)S(1)}, u32[]{:S(2)}, u32[]{:S(2)}) async-start(bf16[8,24,256]{2,1,0:T(8,128)(2,1)} %pieces.1), calls=%async_computation | async-start | bytes 196608 | tf_op jit(solution)/shard_map/all_to_all | solution.py:295
  5.7 39.6 %copy-start = (bf16[2,1,512,768]{3,2,1,0:T(8,128)(2,1)S(1)}, bf16[2,1,512,768]{3,2,1,0:T(8,128)(2,1)}, u32[]{:S(2)}) copy-start(bf16[2,1,512,768]{3,2,1,0:T(8,128)(2,1)} %param.7) | copy-start | bytes 4718596
  5.8 39.6 %copy-start.1 = (bf16[1,768,1024]{2,1,0:T(8,128)(2,1)S(1)}, bf16[1,768,1024]{2,1,0:T(8,128)(2,1)}, u32[]{:S(2)}) copy-start(bf16[1,768,1024]{2,1,0:T(8,128)(2,1)} %param.12) | copy-start | bytes 4718596
  5.8 39.6 %copy-start.4 = (s32[32,1]{0,1:T(1,128)S(1)}, s32[32,1]{0,1:T(1,128)}, u32[]{:S(2)}) copy-start(s32[32,1]{0,1:T(1,128)} %param.11) | copy-start | bytes 388
  11.5 39.6 %collective-permute-start.1 = (bf16[1024,768]{1,0:T(8,128)(2,1)}, bf16[1024,768]{1,0:T(8,128)(2,1)S(1)}, u32[]{:S(2)}, u32[]{:S(2)}) collective-permute-start(bf16[1024,768]{1,0:T(8,128)(2,1)} %outgoing.1), channel_id=1, source_target_pairs={{0,1},{1,0},{2,3},{3,2},{4,5},{5,4},{6,7},{7,6},{8,9},{9,8},{10,11... | collective-permute-start | bytes 4718600 | tf_op jit(solution)/shard_map/ppermute | solution.py:298
  41.2 4.2 %collective-permute-start = (bf16[8,192,256]{2,1,0:T(8,128)(2,1)S(1)}, bf16[8,192,256]{2,1,0:T(8,128)(2,1)S(1)}, u32[]{:S(2)}, u32[]{:S(2)}) collective-permute-start(bf16[8,192,256]{2,1,0:T(8,128)(2,1)S(1)} %all_gather.3.mine_ref), channel_id=1, source_target_pairs={{0,16},{16,0},{32,48},{48,32},{64,80},{80,64},{96,112},{112,96},{1... | collective-permute-start | bytes 2359304 | tf_op jit(solution)/shard_map/ppermute | solution.py:300
  53.0 11.9 %copy-start.5 = (s32[32]{0:T(128)S(1)}, s32[32]{0:T(128)}, u32[]{:S(2)}) copy-start(s32[32]{0:T(128)} %param.10) | copy-start | bytes 388
  53.1 12.2 %copy-start.2 = (bf16[2,1,32,6144]{3,2,1,0:T(8,128)(2,1)S(1)}, bf16[2,1,32,6144]{3,2,1,0:T(8,128)(2,1)}, u32[]{:S(2)}) copy-start(bf16[2,1,32,6144]{3,2,1,0:T(8,128)(2,1)} %param.8) | copy-start | bytes 2359300
  53.1 41.1 %all-to-all-start.1 = ((bf16[16,64,512]{2,1,0:T(8,128)(2,1)}), bf16[16,64,512]{2,1,0:T(8,128)(2,1)S(1)}, u32[]{:S(2)}, u32[]{:S(2)}) async-start(bf16[16,64,512]{2,1,0:T(8,128)(2,1)} %pair.1), calls=%async_computation.1 | async-start | bytes 2097152 | tf_op jit(solution)/shard_map/all_to_all | solution.py:312
  65.3 1.2 %copy-start.3 = (bf16[1,32,16,1024]{3,2,1,0:T(8,128)(2,1)S(1)}, bf16[1,32,16,1024]{3,2,1,0:T(8,128)(2,1)}, u32[]{:S(2)}) copy-start(bf16[1,32,16,1024]{3,2,1,0:T(8,128)(2,1)} %param.9) | copy-start | bytes 3145732

commit v7 on v4

--- a/solution.py
+++ b/solution.py
@@ -134,6 +134,7 @@
     return out.reshape(steps, rows, width)
 
 CHUNK = 256
+PAIR = 128
 
 
 def pieces_kernel(update_ref, out_ref):
@@ -238,13 +239,13 @@
     wide = far_ref.shape[1]
     steps, shards = pair_ref.shape[:2]
     fresh = jnp.max(fresh_ref[...]) == 1
-    blocks = CHUNK // (steps * pair_ref.shape[2])
+    blocks = PAIR // (steps * pair_ref.shape[2])
 
     def rows(i, cols):
         return jnp.concatenate([pair_ref[s, i + b, :, cols] for b in range(blocks) for s in range(steps)], 0)
 
     def send(i, out):
-        out = out + part_ref[i * CHUNK // blocks : (i + blocks) * CHUNK // blocks]
+        out = out + part_ref[i * PAIR // blocks : (i + blocks) * PAIR // blocks]
         held[i : i + blocks] = out.astype(held.dtype).reshape(blocks, -1, wide)
         pltpu.make_async_copy(held.at[i : i + blocks], out_ref.at[i : i + blocks], sems.at[i // blocks]).start()
 
@@ -301,7 +302,7 @@
     part, far, fresh = call(own_kernel, [SM] + [VM] * 4, [VM] * 3, part, [pltpu.VMEM((width, wide), kind)], "own")(
         served, hidden.reshape(steps, shards, local, width), resident[0], mine, other
     )
-    scratch = [pltpu.VMEM(shape, kind), pltpu.SemaphoreType.DMA((steps * rows // CHUNK,))]
+    scratch = [pltpu.VMEM(shape, kind), pltpu.SemaphoreType.DMA((steps * rows // PAIR,))]
     partial = call(pair_kernel, [VM] * 4, ANY, pltpu.HBM(shape, kind), scratch, "pair")(
         fresh, part, far, pair.reshape(steps, shards, local, width)
     )

time: 97.2 us -> 97.2 us (level)
  no operation moved by 1% of the time
where the time goes in v7:
time: 97.2 us; the launch traced here: 96.8 us
  waiting for transfers between devices  36.2 us (37%)
  blocking collectives  26.1 us (27%)
  starting transfers between devices  20.9 us (22%)
  Pallas kernels  11.5 us (12%)
  local copies, waits for them, and re-layouts  1.42 us (1%)
    all_gather x1, blocking collectives, per_device(): lax.all_gather(got.reshape(-1, wide // 2), 'replica', axis=0, axis_index_...  26.1 us
    all_to_all x1, waiting for transfers between devices, per_device(): summands = lax.all_to_all(partial, 'tensor', 0, 0, tiled=True)  26 us
    all_to_all x1, starting transfers between devices, per_device(): summands = lax.all_to_all(partial, 'tensor', 0, 0, tiled=True)  11.9 us
    ppermute x1, waiting for transfers between devices, per_device(): pair = lax.ppermute(message, 'tensor', [(i, i ^ 1) for i in range(shards)])  4.88 us
    all_to_all x1, starting transfers between devices, per_device(): lax.all_to_all(pieces, both, 0, 0, axis_index_groups=groups, tiled=True)  4.3 us
    all_to_all x1, waiting for transfers between devices, per_device(): lax.all_to_all(pieces, both, 0, 0, axis_index_groups=groups, tiled=True)  3.14 us
    ppermute x1, starting transfers between devices, per_device(): pair = lax.ppermute(message, 'tensor', [(i, i ^ 1) for i in range(shards)])  2.8 us
    pallas_call x1, Pallas kernels, finish(): pl.pallas_call(functools.partial(finish_kernel, steps=steps, rows=rows),...  2.65 us
  transfers between devices with their start and end apart: 4, of which 4 were waited for; matrix products, arithmetic and copies ran while one was open for 1% of the time, Pallas kernels for 6%

profile of v7, /device:TPU:32, one launch (start us, length us, event | category | flops | bytes accessed | tf_op | source)
XLA Modules:
  0.0 96.8 jit_solution(8109821608897631723)
XLA Ops:
  0.0 1.4 %pieces.1 = bf16[8,24,256]{2,1,0:T(8,128)(2,1)} custom-call(bf16[24,1024]{1,0:T(8,128)(2,1)} %bitcast.27), custom_call_target="tpu_custom_call" | custom-call | tf_op jit(solution)/shard_map/pieces/pallas_call | solution.py:291
  1.4 4.3 %all-to-all-start = ((bf16[8,24,256]{2,1,0:T(8,128)(2,1)}), bf16[8,24,256]{2,1,0:T(8,128)(2,1)S(1)}, u32[]{:S(2)}, u32[]{:S(2)}) async-start(bf16[8,24,256]{2,1,0:T(8,128)(2,1)} %pieces.1), calls=%async_computation | async-start | bytes 196608 | tf_op jit(solution)/shard_map/all_to_all | solution.py:292
  5.8 2.6 %outgoing.1 = bf16[1024,768]{1,0:T(8,128)(2,1)} custom-call(s32[32]{0:T(128)} %bitcast.24, bf16[1024,768]{1,0:T(8,128)(2,1)} %bitcast.15, bf16[768,1024]{1,0:T(8,128)(2,1)} %bitcast.17), custom_call_target="tpu_custom_call" | custom-call | tf_op jit(solution)/shard_map/outgoing/pallas_call | solution.py:190
  8.4 3.1 %all-to-all-done = bf16[8,24,256]{2,1,0:T(8,128)(2,1)S(1)} async-done(((bf16[8,24,256]{2,1,0:T(8,128)(2,1)}), bf16[8,24,256]{2,1,0:T(8,128)(2,1)S(1)}, u32[]{:S(2)}, u32[]{:S(2)}) %all-to-all-start) | async-done | bytes 98336 | tf_op jit(solution)/shard_map/all_to_all | solution.py:292
  11.5 2.8 %collective-permute-start.1 = (bf16[1024,768]{1,0:T(8,128)(2,1)}, bf16[1024,768]{1,0:T(8,128)(2,1)S(1)}, u32[]{:S(2)}, u32[]{:S(2)}) collective-permute-start(bf16[1024,768]{1,0:T(8,128)(2,1)} %outgoing.1), channel_id=1, source_target_pairs={{0,1},{1,0},{2,3},{3,2},{4,5},{5,4},{6,7},{7,6},{8,9},{9,8},{10,11... | collective-permute-start | bytes 4718600 | tf_op jit(solution)/shard_map/ppermute | solution.py:295
  14.4 26.1 %all_gather.3.mine_ref = bf16[8,192,256]{2,1,0:T(8,128)(2,1)S(1)} all-gather(bf16[1,192,256]{2,1,0:T(8,128)(2,1)S(1)} %bitcast.26), channel_id=1, replica_groups={{0,32,64,96,128,160,192,224},{16,48,80,112,144,176,208,240},{256,288,32..., dimensions={0}, use_global_device_ids=true | all-gather | bytes 884736 | tf_op jit(solution)/shard_map/all_gather | solution.py:296
  40.4 1.9 %collective-permute-start = (bf16[8,192,256]{2,1,0:T(8,128)(2,1)S(1)}, bf16[8,192,256]{2,1,0:T(8,128)(2,1)S(1)}, u32[]{:S(2)}, u32[]{:S(2)}) collective-permute-start(bf16[8,192,256]{2,1,0:T(8,128)(2,1)S(1)} %all_gather.3.mine_ref), channel_id=1, source_target_pairs={{0,16},{16,0},{32,48},{48,32},{64,80},{80,64},{96,112},{112,96},{1... | collective-permute-start | bytes 2359304 | tf_op jit(solution)/shard_map/ppermute | solution.py:297
  42.4 2.2 %collective-permute-done.other_ref = bf16[8,192,256]{2,1,0:T(8,128)(2,1)S(1)} collective-permute-done((bf16[8,192,256]{2,1,0:T(8,128)(2,1)S(1)}, bf16[8,192,256]{2,1,0:T(8,128)(2,1)S(1)}, u32[]{:S(2)}, u32[]{:S(2)}) %collective-permute-start) | collective-permute-done | bytes 786464 | tf_op jit(solution)/shard_map/ppermute | solution.py:297
  44.6 1.6 %own.1 = (f32[1024,512]{1,0:T(8,128)S(1)}, bf16[768,512]{1,0:T(8,128)(2,1)S(1)}, s32[8,128]{1,0:T(8,128)S(1)}) custom-call(s32[32]{0:T(128)S(1)} %bitcast.25, bf16[2,16,32,768]{3,2,1,0:T(8,128)(2,1)S(1)} %bitcast.16, bf16[768,1024]{1,0:T(8,128)(2,1)S(1)} %bitcast.18, bf16[8,192,256]{2,1,0:T(8,128)(2,1)S(1)} %all_gather.3.mine_ref, ...), custom_call_target="tpu_custom_call" | custom-call | tf_op jit(solution)/shard_map/own/pallas_call | solution.py:302
  46.2 4.9 %collective-permute-done.1 = bf16[1024,768]{1,0:T(8,128)(2,1)S(1)} collective-permute-done((bf16[1024,768]{1,0:T(8,128)(2,1)}, bf16[1024,768]{1,0:T(8,128)(2,1)S(1)}, u32[]{:S(2)}, u32[]{:S(2)}) %collective-permute-start.1) | collective-permute-done | bytes 1572896 | tf_op jit(solution)/shard_map/ppermute | solution.py:295
  51.1 1.9 %pair.1 = bf16[16,64,512]{2,1,0:T(8,128)(2,1)} custom-call(s32[8,128]{1,0:T(8,128)S(1)} %get-tuple-element.11.fresh_ref, f32[1024,512]{1,0:T(8,128)S(1)} %get-tuple-element.12.part_ref, bf16[768,512]{1,0:T(8,128)(2,1)S(1)} %get-tuple-element.13.far_ref, bf16[2,16,32,768]{3,2,1,0:T(8,128)(2,1)S(1)} %bitcast.22), custom_call_target="tpu_custom_call" | custom-call | tf_op jit(solution)/shard_map/pair/pallas_call | solution.py:306
  53.0 0.0 copy-start.5
  53.0 0.0 copy-start.2
  53.1 11.9 %all-to-all-start.1 = ((bf16[16,64,512]{2,1,0:T(8,128)(2,1)}), bf16[16,64,512]{2,1,0:T(8,128)(2,1)S(1)}, u32[]{:S(2)}, u32[]{:S(2)}) async-start(bf16[16,64,512]{2,1,0:T(8,128)(2,1)} %pair.1), calls=%async_computation.1 | async-start | bytes 2097152 | tf_op jit(solution)/shard_map/all_to_all | solution.py:309
  65.0 0.1 add.69
  65.1 0.1 add.71
  65.2 0.1 and_select_fusion.bias_ref
  65.3 1.2 %copy-done.3 = bf16[1,32,16,1024]{3,2,1,0:T(8,128)(2,1)S(1)} copy-done((bf16[1,32,16,1024]{3,2,1,0:T(8,128)(2,1)S(1)}, bf16[1,32,16,1024]{3,2,1,0:T(8,128)(2,1)}, u32[]{:S(2)}) %copy-start.3) | copy-done | bytes 1048600
  66.5 1.2 %cache_part.1.acc_ref = f32[3120,128]{1,0:T(8,128)S(1)} custom-call(bf16[64,6144]{1,0:T(8,128)(2,1)S(1)} %bitcast.20, bf16[512,1024]{1,0:T(8,128)(2,1)S(1)} %bitcast.23, f32[32,256]{1,0:T(8,128)S(1)} %and_select_fusion.bias_ref), custom_call_target="tpu_custom_call" | custom-call | flops 402653184 | bytes 6291456 | tf_op jit(solution)/shard_map/cache_part/pallas_call | solution.py:103
  67.8 0.2 fusion.2
  68.0 0.1 pad_maximum_fusion
  68.1 0.1 fusion.1.bias_ref
  68.2 26.0 %all-to-all-done.1 = bf16[16,64,512]{2,1,0:T(8,128)(2,1)S(1)} async-done(((bf16[16,64,512]{2,1,0:T(8,128)(2,1)}), bf16[16,64,512]{2,1,0:T(8,128)(2,1)S(1)}, u32[]{:S(2)}, u32[]{:S(2)}) %all-to-all-start.1) | async-done | bytes 1048608 | tf_op jit(solution)/shard_map/all_to_all | solution.py:309
  94.2 2.6 %finish.1 = bf16[64,6144]{1,0:T(8,128)(2,1)} custom-call(bf16[64,6144]{1,0:T(8,128)(2,1)S(1)} %bitcast.21, bf16[8,2,64,512]{3,2,1,0:T(8,128)(2,1)S(1)} %bitcast.19, f32[64,128]{1,0:T(8,128)S(1)} %get-tuple-element.18.cos_ref, f32[64,128]{1,0:T(8,128)S(1)} %get-tuple-element.19.sin_ref, f32[2,32,64]{2,1,0:T(8,128)S(1)} %fusion.1.bias_ref, ...), custom_call_target="tpu_custom_call" | custom-call | tf_op jit(solution)/shard_map/finish/pallas_call | solution.py:126
  (22 shorter events, 0.1 us)
Async XLA Ops:
  1.4 10.1 %all-to-all-start = ((bf16[8,24,256]{2,1,0:T(8,128)(2,1)}), bf16[8,24,256]{2,1,0:T(8,128)(2,1)S(1)}, u32[]{:S(2)}, u32[]{:S(2)}) async-start(bf16[8,24,256]{2,1,0:T(8,128)(2,1)} %pieces.1), calls=%async_computation | async-start | bytes 196608 | tf_op jit(solution)/shard_map/all_to_all | solution.py:292
  5.7 38.9 %copy-start = (bf16[2,1,512,768]{3,2,1,0:T(8,128)(2,1)S(1)}, bf16[2,1,512,768]{3,2,1,0:T(8,128)(2,1)}, u32[]{:S(2)}) copy-start(bf16[2,1,512,768]{3,2,1,0:T(8,128)(2,1)} %param.7) | copy-start | bytes 4718596
  5.8 38.8 %copy-start.1 = (bf16[1,768,1024]{2,1,0:T(8,128)(2,1)S(1)}, bf16[1,768,1024]{2,1,0:T(8,128)(2,1)}, u32[]{:S(2)}) copy-start(bf16[1,768,1024]{2,1,0:T(8,128)(2,1)} %param.12) | copy-start | bytes 4718596
  5.8 38.8 %copy-start.4 = (s32[32,1]{0,1:T(1,128)S(1)}, s32[32,1]{0,1:T(1,128)}, u32[]{:S(2)}) copy-start(s32[32,1]{0,1:T(1,128)} %param.11) | copy-start | bytes 388
  11.5 39.6 %collective-permute-start.1 = (bf16[1024,768]{1,0:T(8,128)(2,1)}, bf16[1024,768]{1,0:T(8,128)(2,1)S(1)}, u32[]{:S(2)}, u32[]{:S(2)}) collective-permute-start(bf16[1024,768]{1,0:T(8,128)(2,1)} %outgoing.1), channel_id=1, source_target_pairs={{0,1},{1,0},{2,3},{3,2},{4,5},{5,4},{6,7},{7,6},{8,9},{9,8},{10,11... | collective-permute-start | bytes 4718600 | tf_op jit(solution)/shard_map/ppermute | solution.py:295
  40.4 4.2 %collective-permute-start = (bf16[8,192,256]{2,1,0:T(8,128)(2,1)S(1)}, bf16[8,192,256]{2,1,0:T(8,128)(2,1)S(1)}, u32[]{:S(2)}, u32[]{:S(2)}) collective-permute-start(bf16[8,192,256]{2,1,0:T(8,128)(2,1)S(1)} %all_gather.3.mine_ref), channel_id=1, source_target_pairs={{0,16},{16,0},{32,48},{48,32},{64,80},{80,64},{96,112},{112,96},{1... | collective-permute-start | bytes 2359304 | tf_op jit(solution)/shard_map/ppermute | solution.py:297
  53.0 11.9 %copy-start.5 = (s32[32]{0:T(128)S(1)}, s32[32]{0:T(128)}, u32[]{:S(2)}) copy-start(s32[32]{0:T(128)} %param.10) | copy-start | bytes 388
  53.0 12.2 %copy-start.2 = (bf16[2,1,32,6144]{3,2,1,0:T(8,128)(2,1)S(1)}, bf16[2,1,32,6144]{3,2,1,0:T(8,128)(2,1)}, u32[]{:S(2)}) copy-start(bf16[2,1,32,6144]{3,2,1,0:T(8,128)(2,1)} %param.8) | copy-start | bytes 2359300
  53.1 41.1 %all-to-all-start.1 = ((bf16[16,64,512]{2,1,0:T(8,128)(2,1)}), bf16[16,64,512]{2,1,0:T(8,128)(2,1)S(1)}, u32[]{:S(2)}, u32[]{:S(2)}) async-start(bf16[16,64,512]{2,1,0:T(8,128)(2,1)} %pair.1), calls=%async_computation.1 | async-start | bytes 2097152 | tf_op jit(solution)/shard_map/all_to_all | solution.py:309
  65.3 1.2 %copy-start.3 = (bf16[1,32,16,1024]{3,2,1,0:T(8,128)(2,1)S(1)}, bf16[1,32,16,1024]{3,2,1,0:T(8,128)(2,1)}, u32[]{:S(2)}) copy-start(bf16[1,32,16,1024]{3,2,1,0:T(8,128)(2,1)} %param.9) | copy-start | bytes 3145732
